TPU v7x, 256 devices: a whole 4x4x8 slice. The times are simulated.
256 devices in a mesh: freq: 16 (over y_hi, z), sens: 8 (over x, y_lo), op: 2 (over core).
Axes of the slice: x: 4, y: 4 (y_hi: 2, y_lo: 2; y = y_hi * 2 + y_lo), z: 8, core: 2. Of those that a mesh axis runs over, the one named last changes fastest.
Arguments:
- tensor: bfloat16 [8, 16384, 4096], P('op', 'freq', 'sens'), may hold values from -768 to 768
- b_start: bfloat16 [4096, 256], P(('sens', 'freq', 'op')), may hold values from -0.09375 to 0.09375
- c_factor: bfloat16 [8, 256], P('op'), may hold values from 0.5 to 1.5
Outputs:
- a_factor: float32 [16384, 256], P(('freq', 'sens', 'op'))
- b_factor: float32 [4096, 256], P(('sens', 'freq', 'op'))
All inputs are finite; a program needn't handle non-finite values.
Results may differ from a plain program's by a relative error of at most 0.0031.
Values may be sent and summed in bfloat16 or wider, within the bound.
No kernel may reach another device: no remote copies, remote signals or barrier semaphores. Data moves between devices by JAX's collectives and lax.ppermute only.
A program may use at most 64 MiB of HBM per device.

v0:
```python
import jax
import jax.numpy as jnp
from jax import lax
from jax.sharding import PartitionSpec as P

EPS = 1e-06


def solve_rows(right_rows, gram):
    factor = jnp.linalg.cholesky(gram)
    lower_sol = jax.scipy.linalg.solve_triangular(factor, right_rows.T, lower=True)
    return jax.scipy.linalg.solve_triangular(factor, lower_sol, lower=True, trans=1).T


def shards(tensor, b_start, c_factor):
    freq_count = tensor.shape[1]
    c_float = c_factor.astype(jnp.float32)
    b_part = jnp.dot(b_start.T, b_start, preferred_element_type=jnp.float32)
    c_part = jnp.dot(c_factor.T, c_factor, preferred_element_type=jnp.float32)
    b_gram = lax.psum(b_part, ("freq", "sens", "op"))
    c_gram = lax.psum(c_part, "op")
    b_local = lax.all_gather(b_start, ("freq", "op"), axis=0, tiled=True)
    weights_all = (b_local.astype(jnp.float32)[None, :, :] * c_float[:, None, :]).astype(
        jnp.bfloat16
    )
    partial_value = jnp.einsum(
        "kij,kjr->ir", tensor, weights_all, preferred_element_type=jnp.float32
    )
    owned_rows = lax.psum_scatter(partial_value, ("sens", "op"), scatter_dimension=0, tiled=True)
    a_raw = solve_rows(owned_rows, b_gram * c_gram)
    total_freqs = freq_count * lax.axis_size("freq")
    square_sums = lax.psum(jnp.sum(a_raw * a_raw, axis=0), ("freq", "sens", "op"))
    column_scale = jnp.sqrt(square_sums / total_freqs + EPS)
    a_factor = a_raw / column_scale[None, :]
    local_gram = jnp.dot(
        a_factor.T, a_factor, precision=lax.Precision.HIGHEST, preferred_element_type=jnp.float32
    )
    a_gram = lax.psum(local_gram, ("freq", "sens", "op"))
    a_rows = a_factor.astype(jnp.bfloat16)
    weights = (
        lax.all_gather(a_rows, ("sens", "op"), axis=0, tiled=True).astype(jnp.float32)[None, :, :]
        * c_float[:, None, :]
    ).astype(jnp.bfloat16)
    part_two = jnp.einsum("kij,kir->jr", tensor, weights, preferred_element_type=jnp.float32)
    owned_pairs = lax.psum_scatter(part_two, ("freq", "op"), scatter_dimension=0, tiled=True)
    b_factor = solve_rows(owned_pairs, a_gram * c_gram)
    return (a_factor, b_factor)


def solution(mesh):
    in_specs = (P("op", "freq", "sens"), P(("sens", "freq", "op"), None), P("op", None))
    out_specs = (P(("freq", "sens", "op"), None), P(("sens", "freq", "op"), None))
    return jax.shard_map(shards, mesh=mesh, in_specs=in_specs, out_specs=out_specs, check_vma=False)
```

profile of v0, /device:TPU:1, one launch (start us, length us, event | category | flops | bytes accessed | tf_op | source)
XLA Modules:
  0.0 830.0 jit_solution(12645752245403657713)
XLA Ops:
  8.0 1.7 fusion.37
  9.8 1.7 fusion.38
  12.3 47.1 %all_gather.6 = bf16[512,256]{1,0:T(8,128)(2,1)S(1)} all-gather(bf16[16,256]{1,0:T(8,128)(2,1)} %param.5), channel_id=1, replica_groups=mesh['freq'=16,'sens'=8,'op'=2] {'freq','op'}, dimensions={0}, use_global_device_ids=true | all-gather | bytes 270336 | tf_op jit(solution)/shard_map/all_gather | solution.py:22
  59.6 3.5 convolution_bitcast_fusion
  64.5 203.5 %all-reduce.5.cloned.1.call-done = f32[256,256]{0,1:T(8,128)} async-done(((f32[256,256]{0,1:T(8,128)}), f32[256,256]{0,1:T(8,128)}) %all-reduce.5.cloned.1.call-update) | async-done | bytes 262160 | tf_op jit(solution)/shard_map/psum | solution.py:20
  268.0 32.6 %all-reduce.7.cloned.1.call-done = f32[256,256]{0,1:T(8,128)} async-done(((f32[256,256]{0,1:T(8,128)}), f32[256,256]{0,1:T(8,128)}) %all-reduce.7.cloned.1.call-update) | async-done | bytes 262160 | tf_op jit(solution)/shard_map/psum | solution.py:21
  301.9 11.7 %cholesky.130 = f32[128,128]{1,0:T(8,128)S(1)} custom-call(f32[128,128]{1,0:T(8,128)S(1)} %cholesky.194), custom_call_target="Cholesky" | custom-call | tf_op jit(solution)/shard_map/jit(cholesky)/cholesky | solution.py:10
  313.6 9.8 %custom-call.25 = f32[1,128,128]{1,2,0:T(8,128)S(1)} custom-call(f32[1,128,128]{2,1,0:T(8,128)S(1)} %get-tuple-element.48), custom_call_target="InvertDiagBlocksLowerTriangular" | custom-call | tf_op jit(solution)/shard_map/jit(cholesky)/cholesky | solution.py:10
  323.9 11.7 %cholesky.147 = f32[128,128]{1,0:T(8,128)S(1)} custom-call(f32[128,128]{1,0:T(8,128)S(1)} %convolution_subtract_fusion.3), custom_call_target="Cholesky" | custom-call | tf_op jit(solution)/shard_map/jit(cholesky)/cholesky | solution.py:10
  337.7 4.2 while.2
  338.6 1.3 bitcast_dynamic-update-slice_fusion.4
  341.9 19.7 %custom-call.22 = f32[2,128,128]{1,2,0:T(8,128)S(1)} custom-call(f32[2,128,128]{2,1,0:T(8,128)S(1)} %get-tuple-element.10), custom_call_target="InvertDiagBlocksLowerTriangular" | custom-call | tf_op jit(solution)/shard_map/jit(_solve_triangular)/triangular_solve | solution.py:12
  364.1 77.4 %psum.30 = f32[256]{0:T(256)S(1)} all-reduce(f32[256]{0:T(256)S(1)} %multiply_reduce_fusion), channel_id=1, replica_groups=mesh['freq'=16,'sens'=8,'op'=2] {'freq','sens','op'}, use_global_device_ids=true, to_apply=%region_8.10 | all-reduce | flops 256 | bytes 2048 | tf_op jit(solution)/shard_map/psum | solution.py:32
  443.3 19.4 %all_gather.7 = bf16[1024,256]{1,0:T(8,128)(2,1)S(1)} all-gather(bf16[64,256]{1,0:T(8,128)(2,1)S(1)} %get-tuple-element.35), channel_id=1, replica_groups=mesh['freq'=16,'sens'=8,'op'=2] {'sens','op'}, dimensions={0}, use_global_device_ids=true | all-gather | bytes 557056 | tf_op jit(solution)/shard_map/all_gather | solution.py:41
  463.1 3.5 fusion.3
  467.6 239.6 %all-reduce.9.cloned.1.call-done = f32[256,256]{0,1:T(8,128)} async-done(((f32[256,256]{0,1:T(8,128)}), f32[256,256]{0,1:T(8,128)}) %all-reduce.9.cloned.1.call-update) | async-done | bytes 262160 | tf_op jit(solution)/shard_map/psum | solution.py:38
  708.3 11.7 %cholesky.164 = f32[128,128]{1,0:T(8,128)S(1)} custom-call(f32[128,128]{1,0:T(8,128)S(1)} %cholesky.197), custom_call_target="Cholesky" | custom-call | tf_op jit(solution)/shard_map/jit(cholesky)/cholesky | solution.py:10
  720.1 9.8 %custom-call.26 = f32[1,128,128]{1,2,0:T(8,128)S(1)} custom-call(f32[1,128,128]{2,1,0:T(8,128)S(1)} %get-tuple-element.44), custom_call_target="InvertDiagBlocksLowerTriangular" | custom-call | tf_op jit(solution)/shard_map/jit(cholesky)/cholesky | solution.py:10
  730.4 11.7 %cholesky.181 = f32[128,128]{1,0:T(8,128)S(1)} custom-call(f32[128,128]{1,0:T(8,128)S(1)} %convolution_subtract_fusion.1), custom_call_target="Cholesky" | custom-call | tf_op jit(solution)/shard_map/jit(cholesky)/cholesky | solution.py:10
  744.8 4.3 while.3
  745.7 1.3 bitcast_dynamic-update-slice_fusion.5
  747.8 1.3 bitcast_dynamic-update-slice_fusion.5
  749.1 19.7 %custom-call.23 = f32[2,128,128]{1,2,0:T(8,128)S(1)} custom-call(f32[2,128,128]{2,1,0:T(8,128)S(1)} %get-tuple-element.18), custom_call_target="InvertDiagBlocksLowerTriangular" | custom-call | tf_op jit(solution)/shard_map/jit(_solve_triangular)/triangular_solve | solution.py:12
  768.8 51.2 %reduce-scatter.9.cloned.1.call-done = f32[16,256]{1,0:T(8,128)} async-done(((f32[512,256]{1,0:T(8,128)}), f32[16,256]{1,0:T(8,128)}) %reduce-scatter.9.cloned.1.call-update) | async-done | bytes 16400
  (73 shorter events, 20.3 us)
Async XLA Ops:
  8.0 260.0 %all-reduce.5.cloned.1.call-start = ((), (), s32[]{:S(2)}) async-start(), calls=%async_computation.2 | async-start | bytes 524288 | tf_op jit(solution)/shard_map/psum | solution.py:20
  9.8 290.8 %all-reduce.7.cloned.1.call-start = ((), (), s32[]{:S(2)}) async-start(), calls=%async_computation.3 | async-start | bytes 524288 | tf_op jit(solution)/shard_map/psum | solution.py:21
  11.5 350.1 %reduce-scatter.7.cloned.1.call-start = ((), (), s32[]{:S(2)}) async-start(), calls=%async_computation.5 | async-start | bytes 1114112
  64.4 642.7 %all-reduce.9.cloned.1.call-start = ((), (), s32[]{:S(2)}) async-start(), calls=%async_computation.4 | async-start | bytes 524288 | tf_op jit(solution)/shard_map/psum | solution.py:38
  463.0 244.2 %copy-start = (f32[256,256]{0,1:T(8,128)S(1)}, f32[256,256]{0,1:T(8,128)}, u32[]{:S(2)}) copy-start(f32[256,256]{0,1:T(8,128)} %all-reduce.7.cloned.1.call-done) | copy-start | bytes 786436
  463.0 357.0 %reduce-scatter.9.cloned.1.call-start = ((), (), s32[]{:S(2)}) async-start(), calls=%async_computation.6 | async-start | bytes 540672
Sparse Core Ops, SparseCore 0:
  15.2 252.7 all-reduce.4
  270.7 29.8 all-reduce.6
  463.1 243.9 all-reduce.8
  711.0 108.9 reduce-scatter.8
Sparse Core Ops, SparseCore 1:
  64.5 54.3 reduce-scatter.6
where the time goes:
time: 835 us; the launch traced here: 830 us
  waiting for transfers between devices  527 us (63%)
  blocking collectives  144 us (17%)
  other arithmetic  112 us (13%)
  between operations  18 us (2%)
  matrix products  15.3 us (2%)
  local copies, waits for them, and re-layouts  12.8 us (2%)
    psum x1, waiting for transfers between devices, shards(): a_gram = lax.psum(local_gram, ('freq', 'sens', 'op'))  240 us
    psum x1, waiting for transfers between devices, shards(): b_gram = lax.psum(b_part, ('freq', 'sens', 'op'))  203 us
    psum x1, blocking collectives, shards(): lax.psum(jnp.sum(a_raw * a_raw, axis=0), ('freq', 'sens', 'op'))  77.4 us
    another operation x13, other arithmetic, solve_rows(): factor = jnp.linalg.cholesky(gram)  68.6 us
    unnamed x7, waiting for transfers between devices  51.3 us
    all_gather x1, blocking collectives, shards(): b_local = lax.all_gather(b_start, ('freq', 'op'), axis=0, tiled=True)  47.1 us
    another operation x5, other arithmetic, solve_rows(): jax.scipy.linalg.solve_triangular(factor, lower_sol, lower=True, trans=1)  39.4 us
    psum x1, waiting for transfers between devices, shards(): c_gram = lax.psum(c_part, 'op')  32.6 us
  transfers between devices with their start and end apart: 5, of which 4 were waited for; matrix products, arithmetic and copies ran while one was open for 16% of the time, Pallas kernels for 0%

commit v1 on v0

v1 whole, which is shorter than its diff:
```python
import functools

import jax
import jax.numpy as jnp
from jax import lax
from jax.experimental import pallas as pl
from jax.experimental.pallas import tpu as pltpu
from jax.sharding import PartitionSpec as P

EPS = 1e-06
F32 = jnp.float32
BF16 = jnp.bfloat16
HIGH = lax.Precision.HIGHEST
WHOLE = pl.BlockSpec(memory_space=pltpu.VMEM)


def tree_sum(terms):
    while len(terms) > 1:
        pairs = [terms[i] + terms[i + 1] for i in range(0, len(terms) - 1, 2)]
        terms = pairs + terms[len(terms) - len(terms) % 2 :]
    return terms[0]


def sweep(ref):
    tile = (8, 128)
    lane = lax.broadcasted_iota(jnp.int32, tile, 1)
    sub = lax.broadcasted_iota(jnp.int32, tile, 0)

    def step(k, carry):
        row = ref[k]
        from_block = lane - k * 8
        in_block = (from_block >= 0) & (from_block < 8)

        def column(block, j):
            return jnp.take_along_axis(block, jnp.full(tile, k * 8 + j, jnp.int32), axis=1)

        columns = [column(row, j) for j in range(8)]
        d = {}
        for i in range(8):
            for j in range(i + 1):
                d[i, j] = jnp.broadcast_to(columns[j][i : i + 1, :], tile)

        def entry(i, j):
            return d[max(i, j), min(i, j)]

        for p in range(8):
            inverse = 1.0 / d[p, p]
            pivots = [entry(i, p) for i in range(8)]
            scaled = [pivots[i] * inverse for i in range(8)]
            for i in range(8):
                for j in range(i + 1):
                    if i != p and j != p:
                        d[i, j] = d[i, j] - scaled[i] * pivots[j]
            for i in range(8):
                if i != p:
                    d[max(i, p), min(i, p)] = scaled[i]
            d[p, p] = -inverse
        source = jnp.where(in_block, jnp.where(from_block == sub, 1.0, 0.0), -row)
        sources = [jnp.broadcast_to(source[j : j + 1, :], tile) for j in range(8)]
        rows = [tree_sum([entry(i, j) * sources[j] for j in range(8)]) for i in range(8)]
        new_row = rows[0]
        for i in range(1, 8):
            new_row = jnp.where(sub == i, rows[i], new_row)
        for b in range(16):
            block = ref[b]
            change = tree_sum([column(block, j) * rows[j] for j in range(8)])
            ref[b] = jnp.where(in_block, 0.0, block) - change
        ref[k] = new_row
        return carry

    lax.fori_loop(0, 16, step, 0)


def dot(a, b):
    return jnp.dot(a, b, precision=HIGH, preferred_element_type=F32)


def dot_tn(a, b):
    return lax.dot_general(a, b, (((0,), (0,)), ((), ())), precision=HIGH, preferred_element_type=F32)


def dot_nt(a, b):
    return lax.dot_general(a, b, (((1,), (1,)), ((), ())), precision=HIGH, preferred_element_type=F32)


def invert(gram, inverse_ref, block_ref):
    g12 = gram[0:128, 128:256]
    block_ref[...] = gram[0:128, 0:128].reshape(16, 8, 128)
    sweep(block_ref)
    x = -block_ref[...].reshape(128, 128)
    b = dot(x, g12)
    block_ref[...] = (gram[128:256, 128:256] - dot_tn(g12, b)).reshape(16, 8, 128)
    sweep(block_ref)
    y = -block_ref[...].reshape(128, 128)
    z12 = -dot(b, y)
    inverse_ref[0:128, 0:128] = x - dot_nt(z12, b)
    inverse_ref[0:128, 128:256] = z12
    inverse_ref[128:256, 0:128] = z12.T
    inverse_ref[128:256, 128:256] = y


def gram_inverse_kernel(mine_ref, other_ref, c_ref, out_ref, block_ref):
    gram = (mine_ref[...] + other_ref[...]) * dot_tn(c_ref[...], c_ref[...])
    invert(gram, out_ref, block_ref)


def gram_inverse(mine, other, c_all):
    return pl.pallas_call(
        gram_inverse_kernel,
        out_shape=jax.ShapeDtypeStruct(mine.shape, F32),
        in_specs=[WHOLE] * 3,
        out_specs=WHOLE,
        scratch_shapes=[pltpu.VMEM((16, 8, 128), F32)],
        cost_estimate=pl.CostEstimate(flops=10**10, bytes_accessed=10**6, transcendentals=0),
        name="gram_inverse",
    )(mine, other, c_all)


def finish_kernel(total, parts_ref, second_ref, raw_ref, c_ref, a_ref, b_ref, inverse_ref, block_ref):
    parts = parts_ref[...]
    size = parts.shape[-1]
    squares = jnp.sum(jnp.sum(parts[:, 16:24, :], axis=0), axis=0, keepdims=True)
    scale = jnp.sqrt(squares / total + EPS)
    a_ref[...] = raw_ref[...] / scale
    first = lax.broadcasted_iota(jnp.int32, (8, size), 0) == 0
    inverse_scale = jnp.where(first, 1.0 / scale, 0.0)
    gram = parts[:, 0:16, :].reshape(size, size) * dot_tn(inverse_scale, inverse_scale)
    gram = gram * dot_tn(c_ref[...], c_ref[...])
    invert(gram, inverse_ref, block_ref)
    b_ref[...] = dot(second_ref[...] / scale, inverse_ref[...])


def finish(parts, second, raw, c_all, total):
    size = raw.shape[1]
    return pl.pallas_call(
        functools.partial(finish_kernel, float(total)),
        out_shape=(jax.ShapeDtypeStruct(raw.shape, F32), jax.ShapeDtypeStruct(second.shape, F32)),
        in_specs=[WHOLE] * 4,
        out_specs=(WHOLE, WHOLE),
        scratch_shapes=[pltpu.VMEM((size, size), F32), pltpu.VMEM((16, 8, 128), F32)],
        cost_estimate=pl.CostEstimate(flops=10**10, bytes_accessed=10**6, transcendentals=0),
        name="finish",
    )(parts, second, raw, c_all)


def exchange(block, axes):
    return lax.all_to_all(block, axes, 0, 0, tiled=True)


def spread(block, axes):
    count = lax.axis_size(axes)
    return exchange(jnp.broadcast_to(block[None], (count,) + block.shape), axes)


def swap(block):
    return lax.ppermute(block, "op", [(0, 1), (1, 0)])


def add_cores(partial):
    core = lax.axis_index("op")
    keep = lax.dynamic_index_in_dim(partial, core, 1, keepdims=False)
    send = lax.dynamic_index_in_dim(partial, 1 - core, 1, keepdims=False)
    return keep + swap(send)


def shards(tensor, b_start, c_factor):
    points, freq_count, pair_count = tensor.shape
    rank = b_start.shape[1]
    freqs, senses = lax.axis_size("freq"), lax.axis_size("sens")
    core, sens = lax.axis_index("op"), lax.axis_index("sens")
    total_freqs = freq_count * freqs
    c_float = c_factor.astype(F32)
    c_all = lax.all_gather(c_factor, "op", axis=0, tiled=True).astype(F32)

    b_local = spread(b_start, ("freq", "op")).reshape(pair_count, rank)
    half = lax.dynamic_slice_in_dim(b_local, core * (pair_count // 2), pair_count // 2, 0)
    b_half = spread(half, "sens").reshape(senses * (pair_count // 2), rank)
    b_mine = lax.dot_general(b_half, b_half, (((0,), (0,)), ((), ())), preferred_element_type=F32)
    inverse_one = gram_inverse(b_mine, swap(b_mine), c_all)

    weights_one = (b_local.astype(F32)[None] * c_float[:, None, :]).astype(BF16)
    part_one = jnp.einsum("kij,kjr->ir", tensor, weights_one, preferred_element_type=F32)
    own = freq_count // (2 * senses)
    owned = add_cores(part_one.reshape(senses, 2, own, rank))
    first = jnp.sum(exchange(owned, "sens"), axis=0)
    a_raw = jnp.dot(first, inverse_one, precision=HIGH, preferred_element_type=F32)

    a_pair = lax.all_gather(a_raw.astype(BF16), "op", axis=0, tiled=True)
    a_rows = spread(a_pair, "sens").reshape(freq_count, rank)
    weights_two = (a_rows.astype(F32)[None] * c_float[:, None, :]).astype(BF16)
    part_two = jnp.einsum("kij,kir->jr", tensor, weights_two, preferred_element_type=F32)
    own_pairs = pair_count // (2 * freqs)
    owned_pairs = add_cores(part_two.reshape(freqs, 2, own_pairs, rank))
    a_part = lax.dot_general(a_rows, a_rows, (((0,), (0,)), ((), ())), preferred_element_type=F32)
    strip = rank // (2 * senses)
    a_strip = lax.dynamic_slice_in_dim(a_part, (sens * 2 + core) * strip, strip, 0)
    squares = jnp.sum((a_raw * a_raw).reshape(own // 8, 8, rank), axis=0)
    along = jnp.concatenate([a_strip, squares], axis=0)
    along = jnp.broadcast_to(along[None], (freqs,) + along.shape)
    summed = jnp.sum(exchange(jnp.concatenate([owned_pairs, along], axis=1), "freq"), axis=0)
    second, strips = summed[:own_pairs], summed[own_pairs:]
    strips = lax.all_gather(strips[None], "op", axis=0, tiled=True)
    parts = spread(strips, "sens").reshape(2 * senses, strip + 8, rank)
    return finish(parts, second, a_raw, c_all, total_freqs)


def solution(mesh):
    in_specs = (P("op", "freq", "sens"), P(("sens", "freq", "op"), None), P("op", None))
    out_specs = (P(("freq", "sens", "op"), None), P(("sens", "freq", "op"), None))
    return jax.shard_map(shards, mesh=mesh, in_specs=in_specs, out_specs=out_specs, check_vma=False)
```

time: 835 us -> 164 us (0.20)
  waiting for transfers between devices: 527 us -> 40 us
  other arithmetic: 112 us -> 1.92 us
  blocking collectives: 144 us -> 35.1 us
  Pallas kernels: 0 us -> 36.1 us
  starting transfers between devices: 0.21 us -> 32.8 us
  between operations: 18 us -> 0.9 us
    psum x3 -> x0, waiting for transfers between devices: 476 us -> none  [the longest x1 240 us: shards(): a_gram = lax.psum(local_gram, ('freq', 'sens', 'op'))]
    another operation x18 -> x0, other arithmetic: 108 us -> none  [the longest x13 68.6 us: solve_rows(): factor = jnp.linalg.cholesky(gram)]
    psum x1 -> x0, blocking collectives: 77.4 us -> none  [shards(): lax.psum(jnp.sum(a_raw * a_raw, axis=0), ('freq', 'sens', 'op'))]
    all_gather x2 -> x3, blocking collectives: 66.6 us -> 11.6 us  [the longest x1 4.93 us: shards(): strips = lax.all_gather(strips[None], 'op', axis=0, tiled=True)]
    unnamed x7 -> x0, waiting for transfers between devices: 51.3 us -> none
    all_to_all x0 -> x5, waiting for transfers between devices: none -> 37.6 us  [exchange(): return lax.all_to_all(block, axes, 0, 0, tiled=True)]
    pallas_call x0 -> x2, Pallas kernels: none -> 36.1 us  [the longest x1 18.2 us: finish(): pl.pallas_call(functools.partial(finish_kernel, float(total)), out_shape=...]
    all_to_all x0 -> x5, starting transfers between devices: none -> 27.5 us  [exchange(): return lax.all_to_all(block, axes, 0, 0, tiled=True)]
  transfers between devices with their start and end apart: 5 -> 8, of which waited for: 4 -> 7; matrix products, arithmetic and copies ran while one was open for 16% -> 5% of each run, Pallas kernels for 0% -> 0%
where the time goes in v1:
time: 164 us
  waiting for transfers between devices  40 us (24%)
  Pallas kernels  36.1 us (22%)
  blocking collectives  35.1 us (21%)
  starting transfers between devices  32.8 us (20%)
  matrix products  9 us (5%)
  local copies, waits for them, and re-layouts  7.93 us (5%)
  other arithmetic  1.92 us (1%)
    all_to_all x5, waiting for transfers between devices, exchange(): return lax.all_to_all(block, axes, 0, 0, tiled=True)  37.6 us
    all_to_all x5, starting transfers between devices, exchange(): return lax.all_to_all(block, axes, 0, 0, tiled=True)  27.5 us
    all_to_all x1, blocking collectives, exchange(): return lax.all_to_all(block, axes, 0, 0, tiled=True)  23.6 us
    pallas_call x1, Pallas kernels, finish(): pl.pallas_call(functools.partial(finish_kernel, float(total)), out_shape=...  18.2 us
    pallas_call x1, Pallas kernels, gram_inverse(): pl.pallas_call(gram_inverse_kernel, out_shape=jax.ShapeDtypeStruct(mine.s...  17.9 us
    ppermute x3, starting transfers between devices, swap(): return lax.ppermute(block, 'op', [(0, 1), (1, 0)])  5.24 us
    all_gather x1, blocking collectives, shards(): strips = lax.all_gather(strips[None], 'op', axis=0, tiled=True)  4.93 us
    all_gather x1, blocking collectives, shards(): a_pair = lax.all_gather(a_raw.astype(BF16), 'op', axis=0, tiled=True)  4.86 us
  transfers between devices with their start and end apart: 8, of which 7 were waited for; matrix products, arithmetic and copies ran while one was open for 5% of the time, Pallas kernels for 0%

profile of v1, /device:TPU:1, one launch (start us, length us, event | category | flops | bytes accessed | tf_op | source)
XLA Modules:
  0.0 163.7 jit_solution(8788190604651100843)
XLA Ops:
  0.6 1.4 broadcast_in_dim.12
  2.1 12.8 %all-to-all-start = ((bf16[32,16,256]{2,1,0:T(8,128)(2,1)}), bf16[32,16,256]{2,1,0:T(8,128)(2,1)S(1)}, u32[]{:S(2)}, u32[]{:S(2)}) async-start(bf16[32,16,256]{2,1,0:T(8,128)(2,1)} %broadcast_in_dim.12), calls=%async_computation | async-start | bytes 524288 | tf_op jit(solution)/shard_map/all_to_all | solution.py:147
  15.5 12.7 %all-to-all-done = bf16[32,16,256]{2,1,0:T(8,128)(2,1)S(1)} async-done(((bf16[32,16,256]{2,1,0:T(8,128)(2,1)}), bf16[32,16,256]{2,1,0:T(8,128)(2,1)S(1)}, u32[]{:S(2)}, u32[]{:S(2)}) %all-to-all-start) | async-done | bytes 262176 | tf_op jit(solution)/shard_map/all_to_all | solution.py:147
  29.6 4.1 %all-to-all-start.2 = ((bf16[8,256,256]{2,1,0:T(8,128)(2,1)}), bf16[8,256,256]{2,1,0:T(8,128)(2,1)S(1)}, u32[]{:S(2)}, u32[]{:S(2)}) async-start(bf16[8,256,256]{2,1,0:T(8,128)(2,1)} %broadcast_in_dim.13), calls=%async_computation.2 | async-start | bytes 2097152 | tf_op jit(solution)/shard_map/all_to_all | solution.py:147
  33.7 3.5 %convolution_bitcast_fusion = f32[1024,256]{0,1:T(8,128)S(1)} fusion(bf16[4,1024,512]{2,1,0:T(8,128)(2,1)} %param.3, f32[4,256]{1,0:T(4,128)S(1)} %convert_element_type.33, f32[512,256]{0,1:T(8,128)S(1)} %copy.21), kind=kOutput, calls=%fused_computation.5 | convolution fusion | flops 1074790400 | bytes 5771264 | tf_op jit(solution)/shard_map/kij,kjr->ir/dot_general | solution.py:182
  37.6 1.9 %collective-permute-start = (f32[8,64,256]{2,1,0:T(8,128)S(1)}, f32[8,64,256]{2,1,0:T(8,128)S(1)}, u32[]{:S(2)}, u32[]{:S(2)}) collective-permute-start(f32[8,64,256]{2,1,0:T(8,128)S(1)} %dynamic-slice_bitcast_fusion), channel_id=1, source_target_pairs={{0,1},{1,0},{2,3},{3,2},{4,5},{5,4},{6,7},{7,6},{8,9},{9,8},{10,11... | collective-permute-start | bytes 1572872 | tf_op jit(solution)/shard_map/ppermute | solution.py:156
  39.4 1.5 collective-permute-done
  41.9 6.1 %all-to-all-done.2 = bf16[8,256,256]{2,1,0:T(8,128)(2,1)S(1)} async-done(((bf16[8,256,256]{2,1,0:T(8,128)(2,1)}), bf16[8,256,256]{2,1,0:T(8,128)(2,1)S(1)}, u32[]{:S(2)}, u32[]{:S(2)}) %all-to-all-start.2) | async-done | bytes 1048608 | tf_op jit(solution)/shard_map/all_to_all | solution.py:147
  48.0 3.7 %all-to-all-start.1 = ((f32[8,64,256]{2,1,0:T(8,128)}), f32[8,64,256]{2,1,0:T(8,128)S(1)}, u32[]{:S(2)}, u32[]{:S(2)}) async-start(f32[8,64,256]{2,1,0:T(8,128)} %bitcast_add_fusion), calls=%async_computation.1 | async-start | bytes 1048576 | tf_op jit(solution)/shard_map/all_to_all | solution.py:147
  52.2 2.1 %collective-permute-start.1 = (f32[256,256]{1,0:T(8,128)S(1)}, f32[256,256]{1,0:T(8,128)S(1)}, u32[]{:S(2)}, u32[]{:S(2)}) collective-permute-start(f32[256,256]{1,0:T(8,128)S(1)} %convolution_bitcast_fusion.2.mine_ref), channel_id=1, source_target_pairs={{0,1},{1,0},{2,3},{3,2},{4,5},{5,4},{6,7},{7,6},{8,9},{9,8},{10,11... | collective-permute-start | bytes 786440 | tf_op jit(solution)/shard_map/ppermute | solution.py:156
  54.3 1.8 %all-gather.1 = bf16[2,4,256]{2,1,0:T(4,128)(2,1)S(1)} all-gather(bf16[1,4,256]{2,1,0:T(4,128)(2,1)S(1)} %bitcast.47), channel_id=1, replica_groups=mesh['freq'=16,'sens'=8,'op'=2] {'op'}, dimensions={0}, use_global_device_ids=true | all-gather | bytes 6144 | tf_op jit(solution)/shard_map/all_gather | solution.py:173
  56.7 2.3 %all-to-all-done.1 = f32[8,64,256]{2,1,0:T(8,128)S(1)} async-done(((f32[8,64,256]{2,1,0:T(8,128)}), f32[8,64,256]{2,1,0:T(8,128)S(1)}, u32[]{:S(2)}, u32[]{:S(2)}) %all-to-all-start.1) | async-done | bytes 524320 | tf_op jit(solution)/shard_map/all_to_all | solution.py:147
  59.8 17.9 %gram_inverse.1 = f32[256,256]{1,0:T(8,128)} custom-call(f32[256,256]{1,0:T(8,128)} %copy-done.1, f32[256,256]{1,0:T(8,128)} %copy-done.4, f32[8,256]{1,0:T(8,128)} %reshape.48.c_ref), custom_call_target="tpu_custom_call" | custom-call | flops 10000000000 | bytes 1000000 | tf_op jit(solution)/shard_map/gram_inverse/pallas_call | solution.py:108
  77.6 1.2 bitcast_reduce_fusion
  78.8 4.9 %all_gather.10 = bf16[128,256]{1,0:T(8,128)(2,1)S(1)} all-gather(bf16[64,256]{1,0:T(8,128)(2,1)S(1)} %convert_element_type.36), channel_id=1, replica_groups=mesh['freq'=16,'sens'=8,'op'=2] {'op'}, dimensions={0}, use_global_device_ids=true | all-gather | bytes 98304 | tf_op jit(solution)/shard_map/all_gather | solution.py:188
  84.5 3.5 %all-to-all-start.3 = ((bf16[8,128,256]{2,1,0:T(8,128)(2,1)}), bf16[8,128,256]{2,1,0:T(8,128)(2,1)S(1)}, u32[]{:S(2)}, u32[]{:S(2)}) async-start(bf16[8,128,256]{2,1,0:T(8,128)(2,1)} %broadcast_in_dim.14), calls=%async_computation.3 | async-start | bytes 1048576 | tf_op jit(solution)/shard_map/all_to_all | solution.py:147
  88.0 9.2 %all-to-all-done.3 = bf16[8,128,256]{2,1,0:T(8,128)(2,1)S(1)} async-done(((bf16[8,128,256]{2,1,0:T(8,128)(2,1)}), bf16[8,128,256]{2,1,0:T(8,128)(2,1)S(1)}, u32[]{:S(2)}, u32[]{:S(2)}) %all-to-all-start.3) | async-done | bytes 524320 | tf_op jit(solution)/shard_map/all_to_all | solution.py:147
  97.6 3.5 %fusion.3 = f32[512,256]{0,1:T(8,128)S(1)} fusion(bf16[4,1024,512]{2,1,0:T(8,128)(2,1)} %param.3, f32[4,256]{1,0:T(4,128)S(1)} %convert_element_type.33, f32[1024,256]{0,1:T(8,128)S(1)} %copy.24), kind=kOutput, calls=%fused_computation.6 | convolution fusion | flops 1075838976 | bytes 5771264 | tf_op jit(solution)/shard_map/kij,kir->jr/dot_general | solution.py:191
  101.4 1.3 collective-permute-start.2
  104.0 23.6 %all_to_all.30 = f32[16,40,256]{2,1,0:T(8,128)S(1)} all-to-all(f32[16,40,256]{2,1,0:T(8,128)S(1)} %pad_maximum_fusion), channel_id=1, replica_groups=mesh['freq'=16,'sens'=8,'op'=2] {'freq'}, dimensions={0} | all-to-all | bytes 1310720 | tf_op jit(solution)/shard_map/all_to_all | solution.py:147
  127.6 4.9 %all-gather = f32[48,256]{1,0:T(8,128)S(1)} all-gather(f32[24,256]{1,0:T(8,128)S(1)} %slice.8), channel_id=2, replica_groups=mesh['freq'=16,'sens'=8,'op'=2] {'op'}, dimensions={0}, use_global_device_ids=true | all-gather | bytes 73728 | tf_op jit(solution)/shard_map/all_gather | solution.py:202
  133.3 3.5 %all-to-all-start.5 = ((f32[8,2,24,256]{3,2,1,0:T(8,128)}), f32[8,2,24,256]{3,2,1,0:T(8,128)S(1)}, u32[]{:S(2)}, u32[]{:S(2)}) async-start(f32[8,2,24,256]{3,2,1,0:T(8,128)} %broadcast_in_dim.17), calls=%async_computation.5 | async-start | bytes 786432 | tf_op jit(solution)/shard_map/all_to_all | solution.py:147
  137.4 7.3 %all-to-all-done.5 = f32[8,2,24,256]{3,2,1,0:T(8,128)S(1)} async-done(((f32[8,2,24,256]{3,2,1,0:T(8,128)}), f32[8,2,24,256]{3,2,1,0:T(8,128)S(1)}, u32[]{:S(2)}, u32[]{:S(2)}) %all-to-all-start.5) | async-done | bytes 393248 | tf_op jit(solution)/shard_map/all_to_all | solution.py:147
  145.5 18.2 %finish.1 = (f32[64,256]{1,0:T(8,128)}, f32[16,256]{1,0:T(8,128)}) custom-call(f32[16,24,256]{2,1,0:T(8,128)} %bitcast.45, f32[16,256]{1,0:T(8,128)} %slice.9.second_ref, f32[64,256]{1,0:T(8,128)} %copy-done.2, f32[8,256]{1,0:T(8,128)} %reshape.48.c_ref), custom_call_target="tpu_custom_call" | custom-call | flops 10000000000 | bytes 1000000 | tf_op jit(solution)/shard_map/finish/pallas_call | solution.py:135
  (39 shorter events, 10.0 us)
Async XLA Ops:
  2.1 26.2 %all-to-all-start = ((bf16[32,16,256]{2,1,0:T(8,128)(2,1)}), bf16[32,16,256]{2,1,0:T(8,128)(2,1)S(1)}, u32[]{:S(2)}, u32[]{:S(2)}) async-start(bf16[32,16,256]{2,1,0:T(8,128)(2,1)} %broadcast_in_dim.12), calls=%async_computation | async-start | bytes 524288 | tf_op jit(solution)/shard_map/all_to_all | solution.py:147
  29.6 18.5 %all-to-all-start.2 = ((bf16[8,256,256]{2,1,0:T(8,128)(2,1)}), bf16[8,256,256]{2,1,0:T(8,128)(2,1)S(1)}, u32[]{:S(2)}, u32[]{:S(2)}) async-start(bf16[8,256,256]{2,1,0:T(8,128)(2,1)} %broadcast_in_dim.13), calls=%async_computation.2 | async-start | bytes 2097152 | tf_op jit(solution)/shard_map/all_to_all | solution.py:147
  37.2 17.1 %copy-start.3 = (bf16[4,256]{1,0:T(4,128)(2,1)S(1)}, bf16[4,256]{1,0:T(4,128)(2,1)}, u32[]{:S(2)}) copy-start(bf16[4,256]{1,0:T(4,128)(2,1)} %param.5) | copy-start | bytes 6148
  37.6 3.4 %collective-permute-start = (f32[8,64,256]{2,1,0:T(8,128)S(1)}, f32[8,64,256]{2,1,0:T(8,128)S(1)}, u32[]{:S(2)}, u32[]{:S(2)}) collective-permute-start(f32[8,64,256]{2,1,0:T(8,128)S(1)} %dynamic-slice_bitcast_fusion), channel_id=1, source_target_pairs={{0,1},{1,0},{2,3},{3,2},{4,5},{5,4},{6,7},{7,6},{8,9},{9,8},{10,11... | collective-permute-start | bytes 1572872 | tf_op jit(solution)/shard_map/ppermute | solution.py:156
  48.0 11.0 %all-to-all-start.1 = ((f32[8,64,256]{2,1,0:T(8,128)}), f32[8,64,256]{2,1,0:T(8,128)S(1)}, u32[]{:S(2)}, u32[]{:S(2)}) async-start(f32[8,64,256]{2,1,0:T(8,128)} %bitcast_add_fusion), calls=%async_computation.1 | async-start | bytes 1048576 | tf_op jit(solution)/shard_map/all_to_all | solution.py:147
  52.2 6.8 %copy-start.1 = (f32[256,256]{1,0:T(8,128)}, f32[256,256]{1,0:T(8,128)S(1)}, u32[]{:S(2)}) copy-start(f32[256,256]{1,0:T(8,128)S(1)} %convolution_bitcast_fusion.2.mine_ref) | copy-start | bytes 786436
  52.2 6.8 %collective-permute-start.1 = (f32[256,256]{1,0:T(8,128)S(1)}, f32[256,256]{1,0:T(8,128)S(1)}, u32[]{:S(2)}, u32[]{:S(2)}) collective-permute-start(f32[256,256]{1,0:T(8,128)S(1)} %convolution_bitcast_fusion.2.mine_ref), channel_id=1, source_target_pairs={{0,1},{1,0},{2,3},{3,2},{4,5},{5,4},{6,7},{7,6},{8,9},{9,8},{10,11... | collective-permute-start | bytes 786440 | tf_op jit(solution)/shard_map/ppermute | solution.py:156
  59.0 0.7 copy-start.4
  78.8 22.4 %copy-start.2 = (f32[64,256]{1,0:T(8,128)}, f32[64,256]{1,0:T(8,128)S(1)}, u32[]{:S(2)}) copy-start(f32[64,256]{1,0:T(8,128)S(1)} %get-tuple-element.3.raw_ref) | copy-start | bytes 196612
  84.5 12.7 %all-to-all-start.3 = ((bf16[8,128,256]{2,1,0:T(8,128)(2,1)}), bf16[8,128,256]{2,1,0:T(8,128)(2,1)S(1)}, u32[]{:S(2)}, u32[]{:S(2)}) async-start(bf16[8,128,256]{2,1,0:T(8,128)(2,1)} %broadcast_in_dim.14), calls=%async_computation.3 | async-start | bytes 1048576 | tf_op jit(solution)/shard_map/all_to_all | solution.py:147
  101.4 2.4 %collective-permute-start.2 = (f32[16,16,256]{2,1,0:T(8,128)S(1)}, f32[16,16,256]{2,1,0:T(8,128)S(1)}, u32[]{:S(2)}, u32[]{:S(2)}) collective-permute-start(f32[16,16,256]{2,1,0:T(8,128)S(1)} %dynamic-slice_bitcast_fusion.1), channel_id=1, source_target_pairs={{0,1},{1,0},{2,3},{3,2},{4,5},{5,4},{6,7},{7,6},{8,9},{9,8},{10,11... | collective-permute-start | bytes 786440 | tf_op jit(solution)/shard_map/ppermute | solution.py:156
  133.3 11.4 %all-to-all-start.5 = ((f32[8,2,24,256]{3,2,1,0:T(8,128)}), f32[8,2,24,256]{3,2,1,0:T(8,128)S(1)}, u32[]{:S(2)}, u32[]{:S(2)}) async-start(f32[8,2,24,256]{3,2,1,0:T(8,128)} %broadcast_in_dim.17), calls=%async_computation.5 | async-start | bytes 786432 | tf_op jit(solution)/shard_map/all_to_all | solution.py:147
  144.7 0.7 copy-start

commit v2 on v0

v2 whole, which is shorter than its diff:
```python
import functools

import jax
import jax.numpy as jnp
from jax import lax
from jax.experimental import pallas as pl
from jax.experimental.pallas import tpu as pltpu
from jax.sharding import PartitionSpec as P

EPS = 1e-06
F32 = jnp.float32
BF16 = jnp.bfloat16
HIGH = lax.Precision.HIGHEST
WHOLE = pl.BlockSpec(memory_space=pltpu.VMEM)
TILE = (8, 128)
PRODUCT_PARAMS = pltpu.CompilerParams(vmem_limit_bytes=51 * 2**20)
PARAMS = pltpu.CompilerParams(vmem_limit_bytes=24 * 2**20)
SCALARS = pl.BlockSpec(memory_space=pltpu.SMEM)
PRODUCT_COST = pl.CostEstimate(flops=2 * 10**9, bytes_accessed=6 * 10**6, transcendentals=0)
SOLVE_COST = pl.CostEstimate(flops=2 * 10**10, bytes_accessed=10**6, transcendentals=0)


def tree_sum(terms):
    while len(terms) > 1:
        pairs = [terms[i] + terms[i + 1] for i in range(0, len(terms) - 1, 2)]
        terms = pairs + terms[len(terms) - len(terms) % 2 :]
    return terms[0]


def column(block, lane):
    return jnp.take_along_axis(block, jnp.full(TILE, lane, jnp.int32), axis=1)


def invert_block(d):
    def entry(i, j):
        return d[max(i, j), min(i, j)]

    for p in range(0, 8, 2):
        q = p + 1
        first, cross, second = d[p, p], d[q, p], d[q, q]
        determinant = first * second - cross * cross
        guess = pl.reciprocal(determinant, approx=True)
        guess = guess * (2.0 - determinant * guess)
        guess = guess * (2.0 - determinant * guess)
        pp, qp, qq = second * guess, -(cross * guess), first * guess
        rest = [i for i in range(8) if i not in (p, q)]
        left = {i: entry(i, p) for i in rest}
        right = {i: entry(i, q) for i in rest}
        left_new = {i: left[i] * pp + right[i] * qp for i in rest}
        right_new = {i: left[i] * qp + right[i] * qq for i in rest}
        for i in rest:
            for j in rest:
                if j <= i:
                    d[i, j] = d[i, j] - (left_new[i] * left[j] + right_new[i] * right[j])
        for i in rest:
            d[max(i, p), min(i, p)] = left_new[i]
            d[max(i, q), min(i, q)] = right_new[i]
        d[p, p], d[q, p], d[q, q] = -pp, -qp, -qq
    return entry


def sweep_panel(ref, start, half, base):
    lane = lax.broadcasted_iota(jnp.int32, TILE, 1)
    sub = lax.broadcasted_iota(jnp.int32, TILE, 0)
    rows = [
        [ref[pl.ds(pl.multiple_of(start + 8 * m, 8), 8), 128 * h : 128 * h + 128] for h in range(2)]
        for m in range(4)
    ]
    for m in range(4):
        from_block = lane - (base + 8 * m)
        in_block = (from_block >= 0) & (from_block < 8)
        columns = [[column(rows[g][half], base + 8 * m + j) for j in range(8)] for g in range(4)]
        d = {
            (i, j): jnp.broadcast_to(columns[m][j][i : i + 1, :], TILE)
            for i in range(8)
            for j in range(i + 1)
        }
        entry = invert_block(d)
        new, spread_rows = [], []
        for h in range(2):
            source = -rows[m][h]
            if h == half:
                source = jnp.where(in_block, jnp.where(from_block == sub, 1.0, 0.0), source)
            sources = [jnp.broadcast_to(source[j : j + 1, :], TILE) for j in range(8)]
            spread_rows.append(
                [tree_sum([entry(i, j) * sources[j] for j in range(8)]) for i in range(8)]
            )
            row = spread_rows[h][0]
            for i in range(1, 8):
                row = jnp.where(sub == i, spread_rows[h][i], row)
            new.append(row)
        for g in range(4):
            if g == m:
                continue
            for h in range(2):
                block = rows[g][h]
                if h == half:
                    block = jnp.where(in_block, 0.0, block)
                rows[g][h] = block - tree_sum([columns[g][j] * spread_rows[h][j] for j in range(8)])
        rows[m] = new
    return jnp.concatenate([jnp.concatenate(row, axis=1) for row in rows], axis=0)


def sweep(ref):
    lane = lax.broadcasted_iota(jnp.int32, (256, 256), 1)
    for half in range(2):

        def step(k, carry):
            start = half * 128 + k * 32
            panel = pl.ds(pl.multiple_of(start, 32), 32)
            old = ref[panel, :]
            new = sweep_panel(ref, start, half, k * 32)
            in_panel = (lane >= start) & (lane < start + 32)
            ref[...] = jnp.where(in_panel, 0.0, ref[...]) - dot_tn(old, new)
            ref[panel, :] = new
            return carry

        lax.fori_loop(0, 4, step, 0)


def dot(a, b):
    return jnp.dot(a, b, precision=HIGH, preferred_element_type=F32)


def dot_tn(a, b):
    return lax.dot_general(a, b, (((0,), (0,)), ((), ())), precision=HIGH, preferred_element_type=F32)


def diagonal_of(gram):
    on_diagonal = lax.broadcasted_iota(jnp.int32, gram.shape, 0) == lax.broadcasted_iota(jnp.int32, gram.shape, 1)
    return jnp.sum(jnp.where(on_diagonal, gram, 0.0), axis=0, keepdims=True)


def diagonal_scale(gram):
    return lax.rsqrt(diagonal_of(gram))


def outer(row):
    first = lax.broadcasted_iota(jnp.int32, (8, row.shape[1]), 0) == 0
    row = jnp.where(first, row, 0.0)
    return dot_tn(row, row)


def gram_inverse_kernel(mine_ref, other_ref, c_ref, out_ref):
    gram = (mine_ref[...] + other_ref[...]) * dot_tn(c_ref[...], c_ref[...])
    scale = outer(diagonal_scale(gram))
    out_ref[...] = gram * scale
    sweep(out_ref)
    out_ref[...] = -out_ref[...] * scale


def gram_inverse(mine, other, c_all):
    return pl.pallas_call(
        gram_inverse_kernel,
        out_shape=jax.ShapeDtypeStruct(mine.shape, F32),
        in_specs=[WHOLE] * 3,
        out_specs=WHOLE,
        cost_estimate=SOLVE_COST,
        compiler_params=PARAMS,
        name="gram_inverse",
    )(mine, other, c_all)


def in_order(mine, other, core):
    first = jnp.where(core == 0, mine, other)
    second = jnp.where(core == 0, other, mine)
    return jnp.concatenate([first[:, None], second[:, None]], axis=1)


def scaled_inverse_kernel(total, core_ref, mine_ref, other_ref, raw_ref, c_ref, a_ref, inverse_ref, before_ref, after_ref):
    size = raw_ref.shape[1]
    gram = in_order(mine_ref[...], other_ref[...], core_ref[0]).reshape(size, size)
    squares = diagonal_of(gram)
    scale = jnp.sqrt(squares / total + EPS)
    a_ref[...] = raw_ref[...] / scale
    gram = gram * dot_tn(c_ref[...], c_ref[...])
    before = diagonal_scale(gram)
    inverse_ref[...] = gram * outer(before)
    sweep(inverse_ref)
    inverse_ref[...] = -inverse_ref[...]
    before_ref[...] = jnp.broadcast_to(before, before_ref.shape)
    after_ref[...] = jnp.broadcast_to(before * scale, after_ref.shape)


def scaled_inverse(core, mine, other, raw, c_all, total):
    size = raw.shape[1]
    row = jax.ShapeDtypeStruct((8, size), F32)
    return pl.pallas_call(
        functools.partial(scaled_inverse_kernel, float(total)),
        out_shape=(jax.ShapeDtypeStruct(raw.shape, F32), jax.ShapeDtypeStruct((size, size), F32), row, row),
        in_specs=[SCALARS] + [WHOLE] * 4,
        out_specs=(WHOLE,) * 4,
        cost_estimate=SOLVE_COST,
        compiler_params=PARAMS,
        name="scaled_inverse",
    )(core, mine, other, raw, c_all)


def first_product_kernel(core_ref, tensor_ref, mine_ref, other_ref, c_ref, keep_ref, send_ref, held_ref, b_ref, arrived):
    core = core_ref[0]
    points, rows, depth = tensor_ref.shape
    owners, own, rank = keep_ref.shape
    steps = arrived.shape[0]
    height = rows // steps

    def load(i):
        part = pl.ds(pl.multiple_of(i * height, height), height)
        return pltpu.make_async_copy(tensor_ref.at[:, part, :], held_ref.at[:, part, :], arrived.at[i])

    for i in range(steps):
        load(i).start()
    b_ref[...] = in_order(mine_ref[...], other_ref[...], core).reshape(b_ref.shape)
    few = owners // steps

    def step(i, carry):
        load(i).wait()
        total = None
        for k in range(points):
            block = held_ref[k, pl.ds(pl.multiple_of(i * height, height), height), :]
            term = jnp.dot(block, b_ref[...], preferred_element_type=F32) * c_ref[k : k + 1, :]
            total = term if total is None else total + term
        total = total.reshape(few, 2, own, rank)
        keep_ref[pl.ds(i * few, few)] = jnp.where(core == 0, total[:, 0], total[:, 1])
        send_ref[pl.ds(i * few, few)] = jnp.where(core == 0, total[:, 1], total[:, 0])
        return carry

    lax.fori_loop(0, steps, step, 0)


def first_product(core, tensor, mine, other, c_all, owners):
    points, rows, depth = tensor.shape
    rank = mine.shape[-1]
    part = jax.ShapeDtypeStruct((owners, rows // (2 * owners), rank), F32)
    return pl.pallas_call(
        first_product_kernel,
        out_shape=(part, part),
        in_specs=[SCALARS, pl.BlockSpec(memory_space=pl.ANY)] + [WHOLE] * 3,
        out_specs=(WHOLE,) * 2,
        scratch_shapes=[
            pltpu.VMEM(tensor.shape, BF16),
            pltpu.VMEM((depth, rank), BF16),
            pltpu.SemaphoreType.DMA((4,)),
        ],
        compiler_params=PRODUCT_PARAMS,
        cost_estimate=PRODUCT_COST,
        name="first_product",
    )(core, tensor, mine, other, c_all)


def second_product_kernel(core_ref, tensor_ref, mine_ref, other_ref, c_ref, keep_ref, send_ref, held_ref, a_ref, sum_ref, arrived):
    core = core_ref[0]
    owners, own, rank = keep_ref.shape

    def load(k):
        return pltpu.make_async_copy(tensor_ref.at[k], held_ref.at[k], arrived.at[k])

    for k in range(tensor_ref.shape[0]):
        load(k).start()
    a_rows = in_order(mine_ref[...], other_ref[...], core).reshape(a_ref.shape[1], a_ref.shape[0])
    a_ref[...] = a_rows.T
    sum_ref[...] = jnp.zeros_like(sum_ref)

    def step(k, carry):
        load(k).wait()
        term = jnp.dot(a_ref[...], held_ref[k], preferred_element_type=F32)
        sum_ref[...] += term * jnp.concatenate([c_ref[k]] * (term.shape[1] // 128), axis=1)
        return carry

    lax.fori_loop(0, tensor_ref.shape[0], step, 0)
    total = sum_ref[...].T.reshape(owners, 2, own, rank)
    keep_ref[...] = jnp.where(core == 0, total[:, 0], total[:, 1])
    send_ref[...] = jnp.where(core == 0, total[:, 1], total[:, 0])


def second_product(core, tensor, mine, other, c_columns, owners):
    points, depth, rows = tensor.shape
    rank = mine.shape[-1]
    part = jax.ShapeDtypeStruct((owners, rows // (2 * owners), rank), F32)
    return pl.pallas_call(
        second_product_kernel,
        out_shape=(part, part),
        in_specs=[SCALARS, pl.BlockSpec(memory_space=pl.ANY)] + [WHOLE] * 3,
        out_specs=(WHOLE, WHOLE),
        scratch_shapes=[
            pltpu.VMEM(tensor.shape, BF16),
            pltpu.VMEM((rank, depth), BF16),
            pltpu.VMEM((rank, rows), F32),
            pltpu.SemaphoreType.DMA((points,)),
        ],
        compiler_params=PRODUCT_PARAMS,
        cost_estimate=PRODUCT_COST,
        name="second_product",
    )(core, tensor, mine, other, c_columns)


def solve_kernel(parts_ref, inverse_ref, raw_ref, rows_ref):
    raw = dot(jnp.sum(parts_ref[...], axis=0), inverse_ref[...])
    raw_ref[...] = raw
    rows_ref[...] = jnp.broadcast_to(raw.astype(BF16)[None], rows_ref.shape)


def solve(parts, inverse, copies):
    own = parts.shape[1:]
    return pl.pallas_call(
        solve_kernel,
        out_shape=(jax.ShapeDtypeStruct(own, F32), jax.ShapeDtypeStruct((copies,) + own, BF16)),
        in_specs=[WHOLE] * 2,
        out_specs=(WHOLE,) * 2,
        compiler_params=PARAMS,
        name="solve",
    )(parts, inverse)


def sum_spread_kernel(parts_ref, out_ref):
    out_ref[...] = jnp.broadcast_to(jnp.sum(parts_ref[...], axis=0)[None], out_ref.shape)


def sum_spread(parts, copies):
    return pl.pallas_call(
        sum_spread_kernel,
        out_shape=jax.ShapeDtypeStruct((copies,) + parts.shape[1:], F32),
        in_specs=[WHOLE],
        out_specs=WHOLE,
        compiler_params=PARAMS,
        name="sum_spread",
    )(parts)


def last_rows_kernel(parts_ref, inverse_ref, before_ref, after_ref, out_ref):
    rows = jnp.sum(parts_ref[...], axis=0) * before_ref[0:1, :]
    out_ref[...] = dot(rows, inverse_ref[...]) * after_ref[0:1, :]


def last_rows(parts, inverse, before, after):
    return pl.pallas_call(
        last_rows_kernel,
        out_shape=jax.ShapeDtypeStruct(parts.shape[1:], F32),
        in_specs=[WHOLE] * 4,
        out_specs=WHOLE,
        compiler_params=PARAMS,
        name="last_rows",
    )(parts, inverse, before, after)


def gram_strips_kernel(strip_ref, mine_ref, other_ref, out_ref, gram_ref):
    gram = None
    for ref in (mine_ref, other_ref):
        rows = ref[...].reshape(-1, ref.shape[-1])
        term = lax.dot_general(rows, rows, (((0,), (0,)), ((), ())), preferred_element_type=F32)
        gram = term if gram is None else gram + term
    gram_ref[...] = gram
    height = out_ref.shape[1]
    strip = gram_ref[pl.ds(pl.multiple_of(strip_ref[0] * height, height), height), :]
    out_ref[...] = jnp.broadcast_to(strip[None], out_ref.shape)


def gram_strips(strip, mine, other, copies, strips):
    rank = mine.shape[-1]
    return pl.pallas_call(
        gram_strips_kernel,
        out_shape=jax.ShapeDtypeStruct((copies, rank // strips, rank), F32),
        in_specs=[SCALARS, WHOLE, WHOLE],
        out_specs=WHOLE,
        scratch_shapes=[pltpu.VMEM((rank, rank), F32)],
        cost_estimate=pl.CostEstimate(flops=10**9, bytes_accessed=10**6, transcendentals=0),
        compiler_params=PARAMS,
        name="gram_strips",
    )(strip, mine, other)


def add_after_kernel(keep_ref, received_ref, gate_ref, out_ref):
    out_ref[...] = keep_ref[...] + received_ref[...]


def add_after(keep, received, gate):
    return pl.pallas_call(
        add_after_kernel,
        out_shape=jax.ShapeDtypeStruct(keep.shape, F32),
        in_specs=[WHOLE, WHOLE, pl.BlockSpec(memory_space=pl.ANY)],
        out_specs=WHOLE,
        compiler_params=PARAMS,
        name="add_after",
    )(keep, received, gate)


def exchange(block, axes):
    return lax.all_to_all(block, axes, 0, 0, tiled=True)


def spread(block, axes):
    return exchange(jnp.broadcast_to(block[None], (lax.axis_size(axes),) + block.shape), axes)


def swap(block):
    return lax.ppermute(block, "op", [(0, 1), (1, 0)])


def shards(tensor, b_start, c_factor):
    points, freq_count, pair_count = tensor.shape
    rank = b_start.shape[1]
    freqs, senses = lax.axis_size("freq"), lax.axis_size("sens")
    core_id = lax.axis_index("op")
    core = core_id.astype(jnp.int32)[None]
    strip = (lax.axis_index("sens") * 2 + core_id).astype(jnp.int32)[None]
    c_float = c_factor.astype(F32)
    c_all = jnp.concatenate([c_float, swap(c_factor).astype(F32)], axis=0)
    c_columns = jnp.broadcast_to(c_float[:, :, None], (points, rank, 128))

    b_mine = spread(b_start, "freq")
    b_other = swap(b_mine)
    b_half = spread(b_mine.reshape(-1, rank), "sens").reshape(-1, rank)
    b_part = lax.dot_general(b_half, b_half, (((0,), (0,)), ((), ())), preferred_element_type=F32)
    inverse_one = gram_inverse(b_part, swap(b_part), c_all)
    keep, send = first_product(core, tensor, b_mine, b_other, c_all, senses)
    a_raw, a_spread = solve(exchange(keep + swap(send), "sens"), inverse_one, senses)

    a_mine = exchange(a_spread, "sens")
    a_other = swap(a_mine)
    strips = exchange(gram_strips(strip, a_mine, a_other, freqs, 2 * senses), "freq")
    keep, send = second_product(core, tensor, a_mine, a_other, c_columns, freqs)
    strips_mine = exchange(sum_spread(strips, senses), "sens")
    strips_other = swap(strips_mine)
    second = exchange(add_after(keep, swap(send), strips_mine), "freq")
    a_factor, inverse_two, before, after = scaled_inverse(
        core, strips_mine, strips_other, a_raw, c_all, freq_count * freqs
    )
    return a_factor, last_rows(second, inverse_two, before, after)


def solution(mesh):
    in_specs = (P("op", "freq", "sens"), P(("sens", "freq", "op"), None), P("op", None))
    out_specs = (P(("freq", "sens", "op"), None), P(("sens", "freq", "op"), None))
    return jax.shard_map(shards, mesh=mesh, in_specs=in_specs, out_specs=out_specs, check_vma=False)
```

time: 835 us -> 121 us (0.14)
  waiting for transfers between devices: 527 us -> 14.7 us
  other arithmetic: 112 us -> 1.58 us
  blocking collectives: 144 us -> 39 us
  Pallas kernels: 0 us -> 33.9 us
  starting transfers between devices: 0.21 us -> 28 us
  between operations: 18 us -> 0.76 us
  matrix products: 15.3 us -> 0.47 us
  local copies, waits for them, and re-layouts: 12.8 us -> 1.95 us
    psum x3 -> x0, waiting for transfers between devices: 476 us -> none  [the longest x1 240 us: shards(): a_gram = lax.psum(local_gram, ('freq', 'sens', 'op'))]
    another operation x18 -> x0, other arithmetic: 108 us -> none  [the longest x13 68.6 us: solve_rows(): factor = jnp.linalg.cholesky(gram)]
    psum x1 -> x0, blocking collectives: 77.4 us -> none  [shards(): lax.psum(jnp.sum(a_raw * a_raw, axis=0), ('freq', 'sens', 'op'))]
    all_gather x2 -> x0, blocking collectives: 66.6 us -> none  [the longest x1 47.1 us: shards(): b_local = lax.all_gather(b_start, ('freq', 'op'), axis=0, tiled=True)]
    unnamed x7 -> x0, waiting for transfers between devices: 51.3 us -> none
    all_to_all x0 -> x3, blocking collectives: none -> 39 us  [exchange(): return lax.all_to_all(block, axes, 0, 0, tiled=True)]
    pallas_call x0 -> x9, Pallas kernels: none -> 33.9 us  [the longest x1 12.4 us: scaled_inverse(): pl.pallas_call(functools.partial(scaled_inverse_kernel, float(total)), ou...]
    all_to_all x0 -> x4, starting transfers between devices: none -> 16.3 us  [exchange(): return lax.all_to_all(block, axes, 0, 0, tiled=True)]
  transfers between devices with their start and end apart: 5 -> 11, of which waited for: 4 -> 4; matrix products, arithmetic and copies ran while one was open for 16% -> 2% of each run, Pallas kernels for 0% -> 26%
where the time goes in v2:
time: 121 us; the launch traced here: 120 us
  blocking collectives  39 us (32%)
  Pallas kernels  33.9 us (28%)
  starting transfers between devices  28 us (23%)
  waiting for transfers between devices  14.7 us (12%)
  local copies, waits for them, and re-layouts  1.95 us (2%)
  other arithmetic  1.58 us (1%)
    all_to_all x3, blocking collectives, exchange(): return lax.all_to_all(block, axes, 0, 0, tiled=True)  39 us
    all_to_all x4, starting transfers between devices, exchange(): return lax.all_to_all(block, axes, 0, 0, tiled=True)  16.3 us
    all_to_all x4, waiting for transfers between devices, exchange(): return lax.all_to_all(block, axes, 0, 0, tiled=True)  12.9 us
    pallas_call x1, Pallas kernels, scaled_inverse(): pl.pallas_call(functools.partial(scaled_inverse_kernel, float(total)), ou...  12.4 us
    pallas_call x1, Pallas kernels, gram_inverse(): pl.pallas_call(gram_inverse_kernel, out_shape=jax.ShapeDtypeStruct(mine.s...  12.3 us
    ppermute x7, starting transfers between devices, swap(): return lax.ppermute(block, 'op', [(0, 1), (1, 0)])  11.8 us
    pallas_call x1, Pallas kernels, second_product(): pl.pallas_call(second_product_kernel, out_shape=(part, part), in_specs=[S...  3.23 us
    pallas_call x1, Pallas kernels, first_product(): pl.pallas_call(first_product_kernel, out_shape=(part, part), in_specs=[SC...  3.03 us
  transfers between devices with their start and end apart: 11, of which 4 were waited for; matrix products, arithmetic and copies ran while one was open for 2% of the time, Pallas kernels for 26%

profile of v2, /device:TPU:1, one launch (start us, length us, event | category | flops | bytes accessed | tf_op | source)
XLA Modules:
  0.0 120.3 jit_solution(18110888999773540987)
XLA Ops:
  1.3 20.5 %all_to_all.35.mine_ref = bf16[16,16,256]{2,1,0:T(8,128)(2,1)S(1)} all-to-all(bf16[16,16,256]{2,1,0:T(8,128)(2,1)S(1)} %broadcast_in_dim.27), channel_id=1, replica_groups=mesh['freq'=16,'sens'=8,'op'=2] {'freq'}, dimensions={0} | all-to-all | bytes 262144 | tf_op jit(solution)/shard_map/all_to_all | solution.py:387
  21.8 1.0 broadcast_in_dim.29
  22.9 4.1 %all-to-all-start.2 = ((bf16[8,256,256]{2,1,0:T(8,128)(2,1)}), bf16[8,256,256]{2,1,0:T(8,128)(2,1)S(1)}, u32[]{:S(2)}, u32[]{:S(2)}) async-start(bf16[8,256,256]{2,1,0:T(8,128)(2,1)} %broadcast_in_dim.29), calls=%async_computation.2 | async-start | bytes 2097152 | tf_op jit(solution)/shard_map/all_to_all | solution.py:387
  27.0 2.4 %collective-permute-start = (bf16[16,16,256]{2,1,0:T(8,128)(2,1)S(1)}, bf16[16,16,256]{2,1,0:T(8,128)(2,1)S(1)}, u32[]{:S(2)}, u32[]{:S(2)}) collective-permute-start(bf16[16,16,256]{2,1,0:T(8,128)(2,1)S(1)} %all_to_all.35.mine_ref), channel_id=1, source_target_pairs={{0,1},{1,0},{2,3},{3,2},{4,5},{5,4},{6,7},{7,6},{8,9},{9,8},{10,11... | collective-permute-start | bytes 393224 | tf_op jit(solution)/shard_map/ppermute | solution.py:395
  30.8 3.0 %first_product.1 = (f32[8,64,256]{2,1,0:T(8,128)S(1)}, f32[8,64,256]{2,1,0:T(8,128)S(1)}) custom-call(s32[1]{0:T(128)} %bitcast.core_ref, bf16[4,1024,512]{2,1,0:T(8,128)(2,1)} %tensor_ref.3, bf16[16,16,256]{2,1,0:T(8,128)(2,1)S(1)} %all_to_all.35.mine_ref, bf16[16,16,256]{2,1,0:T(8,128)(2,1)S(1)} %collective-permute-done.other_ref, ...), custom_call_target="tpu_custom_call" | custom-call | flops 2000000000 | bytes 6000000 | tf_op jit(solution)/shard_map/first_product/pallas_call | solution.py:234
  34.1 6.6 %all-to-all-done.2 = bf16[8,256,256]{2,1,0:T(8,128)(2,1)S(1)} async-done(((bf16[8,256,256]{2,1,0:T(8,128)(2,1)}), bf16[8,256,256]{2,1,0:T(8,128)(2,1)S(1)}, u32[]{:S(2)}, u32[]{:S(2)}) %all-to-all-start.2) | async-done | bytes 1048608 | tf_op jit(solution)/shard_map/all_to_all | solution.py:387
  41.2 2.9 %collective-permute-start.3 = (f32[256,256]{1,0:T(8,128)S(1)}, f32[256,256]{1,0:T(8,128)S(1)}, u32[]{:S(2)}, u32[]{:S(2)}) collective-permute-start(f32[256,256]{1,0:T(8,128)S(1)} %convolution_bitcast_fusion.mine_ref), channel_id=1, source_target_pairs={{0,1},{1,0},{2,3},{3,2},{4,5},{5,4},{6,7},{7,6},{8,9},{9,8},{10,11... | collective-permute-start | bytes 786440 | tf_op jit(solution)/shard_map/ppermute | solution.py:395
  44.1 0.9 add.7
  45.0 3.5 %all-to-all-start.1 = ((f32[8,64,256]{2,1,0:T(8,128)}), f32[8,64,256]{2,1,0:T(8,128)S(1)}, u32[]{:S(2)}, u32[]{:S(2)}) async-start(f32[8,64,256]{2,1,0:T(8,128)} %add.7), calls=%async_computation.1 | async-start | bytes 1048576 | tf_op jit(solution)/shard_map/all_to_all | solution.py:387
  48.5 12.3 %gram_inverse.1.inverse_ref = f32[256,256]{1,0:T(8,128)S(1)} custom-call(f32[256,256]{1,0:T(8,128)S(1)} %convolution_bitcast_fusion.mine_ref, f32[256,256]{1,0:T(8,128)S(1)} %collective-permute-done.3.other_ref, f32[8,256]{1,0:T(8,128)S(1)} %pad_maximum_fusion.c_ref), custom_call_target="tpu_custom_call" | custom-call | flops 20000000000 | bytes 1000000 | tf_op jit(solution)/shard_map/gram_inverse/pallas_call | solution.py:153
  61.1 10.8 %all_to_all.36.mine_ref = bf16[8,64,256]{2,1,0:T(8,128)(2,1)S(1)} all-to-all(bf16[8,64,256]{2,1,0:T(8,128)(2,1)S(1)} %get-tuple-element.14), channel_id=1, replica_groups=mesh['freq'=16,'sens'=8,'op'=2] {'sens'}, dimensions={0} | all-to-all | bytes 524288 | tf_op jit(solution)/shard_map/all_to_all | solution.py:387
  72.0 1.9 %collective-permute-start.4 = (bf16[8,64,256]{2,1,0:T(8,128)(2,1)S(1)}, bf16[8,64,256]{2,1,0:T(8,128)(2,1)S(1)}, u32[]{:S(2)}, u32[]{:S(2)}) collective-permute-start(bf16[8,64,256]{2,1,0:T(8,128)(2,1)S(1)} %all_to_all.36.mine_ref), channel_id=1, source_target_pairs={{0,1},{1,0},{2,3},{3,2},{4,5},{5,4},{6,7},{7,6},{8,9},{9,8},{10,11... | collective-permute-start | bytes 786440 | tf_op jit(solution)/shard_map/ppermute | solution.py:395
  73.9 1.2 collective-permute-done.4.other_ref
  75.0 1.1 gram_strips.1
  76.1 4.0 %all-to-all-start.4 = ((f32[16,16,256]{2,1,0:T(8,128)}), f32[16,16,256]{2,1,0:T(8,128)S(1)}, u32[]{:S(2)}, u32[]{:S(2)}) async-start(f32[16,16,256]{2,1,0:T(8,128)} %gram_strips.1), calls=%async_computation.4 | async-start | bytes 524288 | tf_op jit(solution)/shard_map/all_to_all | solution.py:387
  80.3 3.2 %second_product.1 = (f32[16,16,256]{2,1,0:T(8,128)S(1)}, f32[16,16,256]{2,1,0:T(8,128)S(1)}) custom-call(s32[1]{0:T(128)} %bitcast.core_ref, bf16[4,1024,512]{2,1,0:T(8,128)(2,1)} %tensor_ref.3, bf16[8,64,256]{2,1,0:T(8,128)(2,1)S(1)} %all_to_all.36.mine_ref, bf16[8,64,256]{2,1,0:T(8,128)(2,1)S(1)} %collective-permute-done.4.other_ref, ...), custom_call_target="tpu_custom_call" | custom-call | flops 2000000000 | bytes 6000000 | tf_op jit(solution)/shard_map/second_product/pallas_call | solution.py:279
  83.5 0.7 collective-permute-start.6
  84.2 6.3 %all-to-all-done.4.parts_ref = f32[16,16,256]{2,1,0:T(8,128)S(1)} async-done(((f32[16,16,256]{2,1,0:T(8,128)}), f32[16,16,256]{2,1,0:T(8,128)S(1)}, u32[]{:S(2)}, u32[]{:S(2)}) %all-to-all-start.4) | async-done | bytes 262176 | tf_op jit(solution)/shard_map/all_to_all | solution.py:387
  90.5 7.6 %all_to_all.37.mine_ref.gate_ref = f32[8,16,256]{2,1,0:T(8,128)S(1)} all-to-all(f32[8,16,256]{2,1,0:T(8,128)S(1)} %sum_spread.1), channel_id=1, replica_groups=mesh['freq'=16,'sens'=8,'op'=2] {'sens'}, dimensions={0} | all-to-all | bytes 262144 | tf_op jit(solution)/shard_map/all_to_all | solution.py:387
  98.2 3.5 %collective-permute-start.5 = (f32[8,16,256]{2,1,0:T(8,128)S(1)}, f32[8,16,256]{2,1,0:T(8,128)S(1)}, u32[]{:S(2)}, u32[]{:S(2)}) collective-permute-start(f32[8,16,256]{2,1,0:T(8,128)S(1)} %all_to_all.37.mine_ref.gate_ref), channel_id=1, source_target_pairs={{0,1},{1,0},{2,3},{3,2},{4,5},{5,4},{6,7},{7,6},{8,9},{9,8},{10,11... | collective-permute-start | bytes 393224 | tf_op jit(solution)/shard_map/ppermute | solution.py:395
  101.6 0.7 add_after.1
  102.4 4.7 %all-to-all-start.6 = ((f32[16,16,256]{2,1,0:T(8,128)}), f32[16,16,256]{2,1,0:T(8,128)S(1)}, u32[]{:S(2)}, u32[]{:S(2)}) async-start(f32[16,16,256]{2,1,0:T(8,128)} %add_after.1), calls=%async_computation.6 | async-start | bytes 524288 | tf_op jit(solution)/shard_map/all_to_all | solution.py:387
  107.1 12.4 %scaled_inverse.1 = (f32[64,256]{1,0:T(8,128)}, f32[256,256]{1,0:T(8,128)S(1)}, f32[8,256]{1,0:T(8,128)S(1)}, f32[8,256]{1,0:T(8,128)S(1)}) custom-call(s32[1]{0:T(128)} %bitcast.core_ref, f32[8,16,256]{2,1,0:T(8,128)S(1)} %all_to_all.37.mine_ref.gate_ref, f32[8,16,256]{2,1,0:T(8,128)S(1)} %collective-permute-done.5.other_ref, ...), custom_call_target="tpu_custom_call" | custom-call | flops 20000000000 | bytes 1000000 | tf_op jit(solution)/shard_map/scaled_inverse/pallas_call | solution.py:188
  119.5 0.9 last_rows.1
  (20 shorter events, 3.3 us)
Async XLA Ops:
  22.9 17.9 %all-to-all-start.2 = ((bf16[8,256,256]{2,1,0:T(8,128)(2,1)}), bf16[8,256,256]{2,1,0:T(8,128)(2,1)S(1)}, u32[]{:S(2)}, u32[]{:S(2)}) async-start(bf16[8,256,256]{2,1,0:T(8,128)(2,1)} %broadcast_in_dim.29), calls=%async_computation.2 | async-start | bytes 2097152 | tf_op jit(solution)/shard_map/all_to_all | solution.py:387
  27.0 3.8 %collective-permute-start = (bf16[16,16,256]{2,1,0:T(8,128)(2,1)S(1)}, bf16[16,16,256]{2,1,0:T(8,128)(2,1)S(1)}, u32[]{:S(2)}, u32[]{:S(2)}) collective-permute-start(bf16[16,16,256]{2,1,0:T(8,128)(2,1)S(1)} %all_to_all.35.mine_ref), channel_id=1, source_target_pairs={{0,1},{1,0},{2,3},{3,2},{4,5},{5,4},{6,7},{7,6},{8,9},{9,8},{10,11... | collective-permute-start | bytes 393224 | tf_op jit(solution)/shard_map/ppermute | solution.py:395
  29.4 1.4 %collective-permute-start.1 = (bf16[4,256]{1,0:T(4,128)(2,1)}, bf16[4,256]{1,0:T(4,128)(2,1)S(1)}, u32[]{:S(2)}, u32[]{:S(2)}) collective-permute-start(bf16[4,256]{1,0:T(4,128)(2,1)} %param.5), channel_id=1, source_target_pairs={{0,1},{1,0},{2,3},{3,2},{4,5},{5,4},{6,7},{7,6},{8,9},{9,8},{10,11... | collective-permute-start | bytes 6152 | tf_op jit(solution)/shard_map/ppermute | solution.py:395
  33.8 10.3 %collective-permute-start.2 = (f32[8,64,256]{2,1,0:T(8,128)S(1)}, f32[8,64,256]{2,1,0:T(8,128)S(1)}, u32[]{:S(2)}, u32[]{:S(2)}) collective-permute-start(f32[8,64,256]{2,1,0:T(8,128)S(1)} %get-tuple-element.13), channel_id=1, source_target_pairs={{0,1},{1,0},{2,3},{3,2},{4,5},{5,4},{6,7},{7,6},{8,9},{9,8},{10,11... | collective-permute-start | bytes 1572872 | tf_op jit(solution)/shard_map/ppermute | solution.py:395
  41.2 7.3 %collective-permute-start.3 = (f32[256,256]{1,0:T(8,128)S(1)}, f32[256,256]{1,0:T(8,128)S(1)}, u32[]{:S(2)}, u32[]{:S(2)}) collective-permute-start(f32[256,256]{1,0:T(8,128)S(1)} %convolution_bitcast_fusion.mine_ref), channel_id=1, source_target_pairs={{0,1},{1,0},{2,3},{3,2},{4,5},{5,4},{6,7},{7,6},{8,9},{9,8},{10,11... | collective-permute-start | bytes 786440 | tf_op jit(solution)/shard_map/ppermute | solution.py:395
  45.0 15.9 %all-to-all-start.1 = ((f32[8,64,256]{2,1,0:T(8,128)}), f32[8,64,256]{2,1,0:T(8,128)S(1)}, u32[]{:S(2)}, u32[]{:S(2)}) async-start(f32[8,64,256]{2,1,0:T(8,128)} %add.7), calls=%async_computation.1 | async-start | bytes 1048576 | tf_op jit(solution)/shard_map/all_to_all | solution.py:387
  60.8 19.2 %copy-start = (bf16[4,256]{1,0:T(4,128)(2,1)S(1)}, bf16[4,256]{1,0:T(4,128)(2,1)}, u32[]{:S(2)}) copy-start(bf16[4,256]{1,0:T(4,128)(2,1)} %param.5) | copy-start | bytes 6148
  72.0 3.1 %collective-permute-start.4 = (bf16[8,64,256]{2,1,0:T(8,128)(2,1)S(1)}, bf16[8,64,256]{2,1,0:T(8,128)(2,1)S(1)}, u32[]{:S(2)}, u32[]{:S(2)}) collective-permute-start(bf16[8,64,256]{2,1,0:T(8,128)(2,1)S(1)} %all_to_all.36.mine_ref), channel_id=1, source_target_pairs={{0,1},{1,0},{2,3},{3,2},{4,5},{5,4},{6,7},{7,6},{8,9},{9,8},{10,11... | collective-permute-start | bytes 786440 | tf_op jit(solution)/shard_map/ppermute | solution.py:395
  76.1 14.4 %all-to-all-start.4 = ((f32[16,16,256]{2,1,0:T(8,128)}), f32[16,16,256]{2,1,0:T(8,128)S(1)}, u32[]{:S(2)}, u32[]{:S(2)}) async-start(f32[16,16,256]{2,1,0:T(8,128)} %gram_strips.1), calls=%async_computation.4 | async-start | bytes 524288 | tf_op jit(solution)/shard_map/all_to_all | solution.py:387
  83.5 18.1 %collective-permute-start.6 = (f32[16,16,256]{2,1,0:T(8,128)S(1)}, f32[16,16,256]{2,1,0:T(8,128)S(1)}, u32[]{:S(2)}, u32[]{:S(2)}) collective-permute-start(f32[16,16,256]{2,1,0:T(8,128)S(1)} %get-tuple-element.18), channel_id=1, source_target_pairs={{0,1},{1,0},{2,3},{3,2},{4,5},{5,4},{6,7},{7,6},{8,9},{9,8},{10,11... | collective-permute-start | bytes 786440 | tf_op jit(solution)/shard_map/ppermute | solution.py:395
  98.2 8.9 %collective-permute-start.5 = (f32[8,16,256]{2,1,0:T(8,128)S(1)}, f32[8,16,256]{2,1,0:T(8,128)S(1)}, u32[]{:S(2)}, u32[]{:S(2)}) collective-permute-start(f32[8,16,256]{2,1,0:T(8,128)S(1)} %all_to_all.37.mine_ref.gate_ref), channel_id=1, source_target_pairs={{0,1},{1,0},{2,3},{3,2},{4,5},{5,4},{6,7},{7,6},{8,9},{9,8},{10,11... | collective-permute-start | bytes 393224 | tf_op jit(solution)/shard_map/ppermute | solution.py:395
  102.4 17.1 %all-to-all-start.6 = ((f32[16,16,256]{2,1,0:T(8,128)}), f32[16,16,256]{2,1,0:T(8,128)S(1)}, u32[]{:S(2)}, u32[]{:S(2)}) async-start(f32[16,16,256]{2,1,0:T(8,128)} %add_after.1), calls=%async_computation.6 | async-start | bytes 524288 | tf_op jit(solution)/shard_map/all_to_all | solution.py:387

commit v3 on v2

--- a/solution.py
+++ b/solution.py
@@ -40,7 +40,6 @@
         first, cross, second = d[p, p], d[q, p], d[q, q]
         determinant = first * second - cross * cross
         guess = pl.reciprocal(determinant, approx=True)
-        guess = guess * (2.0 - determinant * guess)
         guess = guess * (2.0 - determinant * guess)
         pp, qp, qq = second * guess, -(cross * guess), first * guess
         rest = [i for i in range(8) if i not in (p, q)]
@@ -101,6 +100,21 @@
     return jnp.concatenate([jnp.concatenate(row, axis=1) for row in rows], axis=0)
 
 
+def three_parts(x):
+    first = x.astype(BF16)
+    rest = x - first.astype(F32)
+    second = rest.astype(BF16)
+    return first, second, (rest - second.astype(F32)).astype(BF16)
+
+
+def narrow_tn(a, b):
+    a1, a2, a3 = three_parts(a)
+    b1, b2, b3 = three_parts(b)
+    left = jnp.concatenate([a1, a1, a1, a2, a2, a3], axis=0)
+    right = jnp.concatenate([b1, b2, b3, b1, b2, b1], axis=0)
+    return lax.dot_general(left, right, (((0,), (0,)), ((), ())), preferred_element_type=F32)
+
+
 def sweep(ref):
     lane = lax.broadcasted_iota(jnp.int32, (256, 256), 1)
     for half in range(2):
@@ -111,7 +125,7 @@
             old = ref[panel, :]
             new = sweep_panel(ref, start, half, k * 32)
             in_panel = (lane >= start) & (lane < start + 32)
-            ref[...] = jnp.where(in_panel, 0.0, ref[...]) - dot_tn(old, new)
+            ref[...] = jnp.where(in_panel, 0.0, ref[...]) - narrow_tn(old, new)
             ref[panel, :] = new
             return carry
 
@@ -136,29 +150,31 @@
 
 
 def outer(row):
-    first = lax.broadcasted_iota(jnp.int32, (8, row.shape[1]), 0) == 0
-    row = jnp.where(first, row, 0.0)
-    return dot_tn(row, row)
-
-
-def gram_inverse_kernel(mine_ref, other_ref, c_ref, out_ref):
-    gram = (mine_ref[...] + other_ref[...]) * dot_tn(c_ref[...], c_ref[...])
+    rows = jnp.where(lax.broadcasted_iota(jnp.int32, (16, row.shape[1]), 0) == 0, row, 0.0)
+    return narrow_tn(rows, rows)
+
+
+def gram_inverse_kernel(mine_ref, other_ref, out_ref, c_gram_ref):
+    c_gram = mine_ref[1] + other_ref[1]
+    c_gram_ref[...] = c_gram
+    gram = (mine_ref[0] + other_ref[0]) * c_gram
     scale = outer(diagonal_scale(gram))
     out_ref[...] = gram * scale
     sweep(out_ref)
     out_ref[...] = -out_ref[...] * scale
 
 
-def gram_inverse(mine, other, c_all):
+def gram_inverse(mine, other):
+    square = jax.ShapeDtypeStruct(mine.shape[1:], F32)
     return pl.pallas_call(
         gram_inverse_kernel,
-        out_shape=jax.ShapeDtypeStruct(mine.shape, F32),
-        in_specs=[WHOLE] * 3,
-        out_specs=WHOLE,
+        out_shape=(square, square),
+        in_specs=[WHOLE] * 2,
+        out_specs=(WHOLE,) * 2,
+        compiler_params=PARAMS,
         cost_estimate=SOLVE_COST,
-        compiler_params=PARAMS,
         name="gram_inverse",
-    )(mine, other, c_all)
+    )(mine, other)
 
 
 def in_order(mine, other, core):
@@ -167,33 +183,30 @@
     return jnp.concatenate([first[:, None], second[:, None]], axis=1)
 
 
-def scaled_inverse_kernel(total, core_ref, mine_ref, other_ref, raw_ref, c_ref, a_ref, inverse_ref, before_ref, after_ref):
-    size = raw_ref.shape[1]
+def scaled_inverse_kernel(total, core_ref, mine_ref, other_ref, c_ref, inverse_ref, rows_ref):
+    size = c_ref.shape[1]
     gram = in_order(mine_ref[...], other_ref[...], core_ref[0]).reshape(size, size)
     squares = diagonal_of(gram)
     scale = jnp.sqrt(squares / total + EPS)
-    a_ref[...] = raw_ref[...] / scale
-    gram = gram * dot_tn(c_ref[...], c_ref[...])
+    gram = gram * c_ref[...]
     before = diagonal_scale(gram)
     inverse_ref[...] = gram * outer(before)
     sweep(inverse_ref)
     inverse_ref[...] = -inverse_ref[...]
-    before_ref[...] = jnp.broadcast_to(before, before_ref.shape)
-    after_ref[...] = jnp.broadcast_to(before * scale, after_ref.shape)
-
-
-def scaled_inverse(core, mine, other, raw, c_all, total):
-    size = raw.shape[1]
-    row = jax.ShapeDtypeStruct((8, size), F32)
+    rows_ref[...] = jnp.concatenate([before, before * scale, scale] + [scale] * 5, axis=0)
+
+
+def scaled_inverse(core, mine, other, c_gram, total):
+    size = c_gram.shape[1]
     return pl.pallas_call(
         functools.partial(scaled_inverse_kernel, float(total)),
-        out_shape=(jax.ShapeDtypeStruct(raw.shape, F32), jax.ShapeDtypeStruct((size, size), F32), row, row),
-        in_specs=[SCALARS] + [WHOLE] * 4,
-        out_specs=(WHOLE,) * 4,
+        out_shape=(jax.ShapeDtypeStruct((size, size), F32), jax.ShapeDtypeStruct((8, size), F32)),
+        in_specs=[SCALARS] + [WHOLE] * 3,
+        out_specs=(WHOLE,) * 2,
         cost_estimate=SOLVE_COST,
         compiler_params=PARAMS,
         name="scaled_inverse",
-    )(core, mine, other, raw, c_all)
+    )(core, mine, other, c_gram)
 
 
 def first_product_kernel(core_ref, tensor_ref, mine_ref, other_ref, c_ref, keep_ref, send_ref, held_ref, b_ref, arrived):
@@ -211,13 +224,14 @@
         load(i).start()
     b_ref[...] = in_order(mine_ref[...], other_ref[...], core).reshape(b_ref.shape)
     few = owners // steps
+    c_float = c_ref[...].astype(F32)
 
     def step(i, carry):
         load(i).wait()
         total = None
         for k in range(points):
             block = held_ref[k, pl.ds(pl.multiple_of(i * height, height), height), :]
-            term = jnp.dot(block, b_ref[...], preferred_element_type=F32) * c_ref[k : k + 1, :]
+            term = jnp.dot(block, b_ref[...], preferred_element_type=F32) * c_float[k : k + 1, :]
             total = term if total is None else total + term
         total = total.reshape(few, 2, own, rank)
         keep_ref[pl.ds(i * few, few)] = jnp.where(core == 0, total[:, 0], total[:, 1])
@@ -227,7 +241,7 @@
     lax.fori_loop(0, steps, step, 0)
 
 
-def first_product(core, tensor, mine, other, c_all, owners):
+def first_product(core, tensor, mine, other, c_factor, owners):
     points, rows, depth = tensor.shape
     rank = mine.shape[-1]
     part = jax.ShapeDtypeStruct((owners, rows // (2 * owners), rank), F32)
@@ -244,10 +258,10 @@
         compiler_params=PRODUCT_PARAMS,
         cost_estimate=PRODUCT_COST,
         name="first_product",
-    )(core, tensor, mine, other, c_all)
-
-
-def second_product_kernel(core_ref, tensor_ref, mine_ref, other_ref, c_ref, keep_ref, send_ref, held_ref, a_ref, sum_ref, arrived):
+    )(core, tensor, mine, other, c_factor)
+
+
+def second_product_kernel(core_ref, tensor_ref, mine_ref, other_ref, c_ref, keep_ref, send_ref, held_ref, a_ref, sum_ref, column_ref, arrived):
     core = core_ref[0]
     owners, own, rank = keep_ref.shape
 
@@ -259,11 +273,15 @@
     a_rows = in_order(mine_ref[...], other_ref[...], core).reshape(a_ref.shape[1], a_ref.shape[0])
     a_ref[...] = a_rows.T
     sum_ref[...] = jnp.zeros_like(sum_ref)
+    points, rank = c_ref.shape
+    columns = jnp.concatenate([c_ref[...].astype(F32)] * (8 // points), axis=0).T
+    for k in range(points):
+        column_ref[k] = jnp.broadcast_to(columns[:, k : k + 1], (rank, 128))
 
     def step(k, carry):
         load(k).wait()
         term = jnp.dot(a_ref[...], held_ref[k], preferred_element_type=F32)
-        sum_ref[...] += term * jnp.concatenate([c_ref[k]] * (term.shape[1] // 128), axis=1)
+        sum_ref[...] += term * jnp.concatenate([column_ref[k]] * (term.shape[1] // 128), axis=1)
         return carry
 
     lax.fori_loop(0, tensor_ref.shape[0], step, 0)
@@ -272,7 +290,7 @@
     send_ref[...] = jnp.where(core == 0, total[:, 1], total[:, 0])
 
 
-def second_product(core, tensor, mine, other, c_columns, owners):
+def second_product(core, tensor, mine, other, c_factor, owners):
     points, depth, rows = tensor.shape
     rank = mine.shape[-1]
     part = jax.ShapeDtypeStruct((owners, rows // (2 * owners), rank), F32)
@@ -285,12 +303,13 @@
             pltpu.VMEM(tensor.shape, BF16),
             pltpu.VMEM((rank, depth), BF16),
             pltpu.VMEM((rank, rows), F32),
+            pltpu.VMEM((points, rank, 128), F32),
             pltpu.SemaphoreType.DMA((points,)),
         ],
         compiler_params=PRODUCT_PARAMS,
         cost_estimate=PRODUCT_COST,
         name="second_product",
-    )(core, tensor, mine, other, c_columns)
+    )(core, tensor, mine, other, c_factor)
 
 
 def solve_kernel(parts_ref, inverse_ref, raw_ref, rows_ref):
@@ -312,7 +331,7 @@
 
 
 def sum_spread_kernel(parts_ref, out_ref):
-    out_ref[...] = jnp.broadcast_to(jnp.sum(parts_ref[...], axis=0)[None], out_ref.shape)
+    out_ref[...] = jnp.broadcast_to(jnp.sum(parts_ref[...].astype(F32), axis=0)[None], out_ref.shape)
 
 
 def sum_spread(parts, copies):
@@ -326,46 +345,79 @@
     )(parts)
 
 
-def last_rows_kernel(parts_ref, inverse_ref, before_ref, after_ref, out_ref):
-    rows = jnp.sum(parts_ref[...], axis=0) * before_ref[0:1, :]
-    out_ref[...] = dot(rows, inverse_ref[...]) * after_ref[0:1, :]
-
-
-def last_rows(parts, inverse, before, after):
+def last_rows_kernel(parts_ref, raw_ref, inverse_ref, rows_ref, a_ref, b_ref):
+    a_ref[...] = raw_ref[...] * (1.0 / rows_ref[2:3, :])
+    rows = jnp.sum(parts_ref[...], axis=0) * rows_ref[0:1, :]
+    b_ref[...] = dot(rows, inverse_ref[...]) * rows_ref[1:2, :]
+
+
+def last_rows(parts, raw, inverse, rows):
     return pl.pallas_call(
         last_rows_kernel,
-        out_shape=jax.ShapeDtypeStruct(parts.shape[1:], F32),
+        out_shape=(jax.ShapeDtypeStruct(raw.shape, F32), jax.ShapeDtypeStruct(parts.shape[1:], F32)),
         in_specs=[WHOLE] * 4,
+        out_specs=(WHOLE,) * 2,
+        compiler_params=PARAMS,
+        name="last_rows",
+    )(parts, raw, inverse, rows)
+
+
+def gram_strips_kernel(place_ref, rows_ref, keep_ref, send_ref, gram_ref):
+    rows = rows_ref[...].reshape(-1, rows_ref.shape[-1])
+    gram_ref[...] = lax.dot_general(rows, rows, (((0,), (0,)), ((), ())), preferred_element_type=F32)
+    height = keep_ref.shape[0]
+    keep_ref[...] = gram_ref[pl.ds(pl.multiple_of(place_ref[1] * height, height), height), :]
+    send_ref[...] = gram_ref[pl.ds(pl.multiple_of(place_ref[2] * height, height), height), :]
+
+
+def gram_strips(place, rows, strips):
+    rank = rows.shape[-1]
+    return pl.pallas_call(
+        gram_strips_kernel,
+        out_shape=(jax.ShapeDtypeStruct((rank // strips, rank), F32),) * 2,
+        in_specs=[SCALARS, WHOLE],
+        out_specs=(WHOLE,) * 2,
+        scratch_shapes=[pltpu.VMEM((rank, rank), F32)],
+        compiler_params=PARAMS,
+        cost_estimate=pl.CostEstimate(flops=10**9, bytes_accessed=10**6, transcendentals=0),
+        name="gram_strips",
+    )(place, rows)
+
+
+def pair_spread_kernel(mine_ref, other_ref, out_ref):
+    out_ref[...] = jnp.broadcast_to((mine_ref[...] + other_ref[...]).astype(BF16)[None], out_ref.shape)
+
+
+def pair_spread(mine, other, copies):
+    return pl.pallas_call(
+        pair_spread_kernel,
+        out_shape=jax.ShapeDtypeStruct((copies,) + mine.shape, BF16),
+        in_specs=[WHOLE] * 2,
         out_specs=WHOLE,
         compiler_params=PARAMS,
-        name="last_rows",
-    )(parts, inverse, before, after)
-
-
-def gram_strips_kernel(strip_ref, mine_ref, other_ref, out_ref, gram_ref):
-    gram = None
-    for ref in (mine_ref, other_ref):
-        rows = ref[...].reshape(-1, ref.shape[-1])
-        term = lax.dot_general(rows, rows, (((0,), (0,)), ((), ())), preferred_element_type=F32)
-        gram = term if gram is None else gram + term
-    gram_ref[...] = gram
-    height = out_ref.shape[1]
-    strip = gram_ref[pl.ds(pl.multiple_of(strip_ref[0] * height, height), height), :]
-    out_ref[...] = jnp.broadcast_to(strip[None], out_ref.shape)
-
-
-def gram_strips(strip, mine, other, copies, strips):
-    rank = mine.shape[-1]
-    return pl.pallas_call(
-        gram_strips_kernel,
-        out_shape=jax.ShapeDtypeStruct((copies, rank // strips, rank), F32),
-        in_specs=[SCALARS, WHOLE, WHOLE],
+        name="pair_spread",
+    )(mine, other)
+
+
+def rows_grams_kernel(rows_ref, c_ref, gate_ref, out_ref):
+    points, rank = c_ref.shape
+    rows = rows_ref[...].reshape(-1, rank)
+    out_ref[0] = lax.dot_general(rows, rows, (((0,), (0,)), ((), ())), preferred_element_type=F32)
+    own = jnp.concatenate([c_ref[...].astype(F32)] * (16 // points), axis=0)
+    own = jnp.where(lax.broadcasted_iota(jnp.int32, own.shape, 0) < points, own, 0.0).astype(BF16)
+    out_ref[1] = lax.dot_general(own, own, (((0,), (0,)), ((), ())), preferred_element_type=F32)
+
+
+def rows_grams(rows, c_factor, gate):
+    rank = rows.shape[-1]
+    return pl.pallas_call(
+        rows_grams_kernel,
+        out_shape=jax.ShapeDtypeStruct((2, rank, rank), F32),
+        in_specs=[WHOLE, WHOLE, pl.BlockSpec(memory_space=pl.ANY)],
         out_specs=WHOLE,
-        scratch_shapes=[pltpu.VMEM((rank, rank), F32)],
-        cost_estimate=pl.CostEstimate(flops=10**9, bytes_accessed=10**6, transcendentals=0),
-        compiler_params=PARAMS,
-        name="gram_strips",
-    )(strip, mine, other)
+        compiler_params=PARAMS,
+        name="rows_grams",
+    )(rows, c_factor, gate)
 
 
 def add_after_kernel(keep_ref, received_ref, gate_ref, out_ref):
@@ -400,31 +452,28 @@
     rank = b_start.shape[1]
     freqs, senses = lax.axis_size("freq"), lax.axis_size("sens")
     core_id = lax.axis_index("op")
-    core = core_id.astype(jnp.int32)[None]
-    strip = (lax.axis_index("sens") * 2 + core_id).astype(jnp.int32)[None]
-    c_float = c_factor.astype(F32)
-    c_all = jnp.concatenate([c_float, swap(c_factor).astype(F32)], axis=0)
-    c_columns = jnp.broadcast_to(c_float[:, :, None], (points, rank, 128))
+    strip = lax.axis_index("sens") * 2
+    place = jnp.stack([core_id, strip + core_id, strip + 1 - core_id]).astype(jnp.int32)
 
     b_mine = spread(b_start, "freq")
     b_other = swap(b_mine)
-    b_half = spread(b_mine.reshape(-1, rank), "sens").reshape(-1, rank)
-    b_part = lax.dot_general(b_half, b_half, (((0,), (0,)), ((), ())), preferred_element_type=F32)
-    inverse_one = gram_inverse(b_part, swap(b_part), c_all)
-    keep, send = first_product(core, tensor, b_mine, b_other, c_all, senses)
-    a_raw, a_spread = solve(exchange(keep + swap(send), "sens"), inverse_one, senses)
+    b_half = spread(b_mine.reshape(-1, rank), "sens")
+    keep, send = first_product(place, tensor, b_mine, b_other, c_factor, senses)
+    owned = keep + swap(send)
+    grams = rows_grams(b_half, c_factor, owned)
+    inverse_one, c_gram = gram_inverse(grams, swap(grams))
+    a_raw, a_spread = solve(exchange(owned, "sens"), inverse_one, senses)
 
     a_mine = exchange(a_spread, "sens")
+    strip_keep, strip_send = gram_strips(place, a_mine, 2 * senses)
+    strips = exchange(pair_spread(strip_keep, swap(strip_send), freqs), "freq")
     a_other = swap(a_mine)
-    strips = exchange(gram_strips(strip, a_mine, a_other, freqs, 2 * senses), "freq")
-    keep, send = second_product(core, tensor, a_mine, a_other, c_columns, freqs)
+    keep, send = second_product(place, tensor, a_mine, a_other, c_factor, freqs)
     strips_mine = exchange(sum_spread(strips, senses), "sens")
     strips_other = swap(strips_mine)
     second = exchange(add_after(keep, swap(send), strips_mine), "freq")
-    a_factor, inverse_two, before, after = scaled_inverse(
-        core, strips_mine, strips_other, a_raw, c_all, freq_count * freqs
-    )
-    return a_factor, last_rows(second, inverse_two, before, after)
+    inverse_two, rows = scaled_inverse(place, strips_mine, strips_other, c_gram, freq_count * freqs)
+    return last_rows(second, a_raw, inverse_two, rows)
 
 
 def solution(mesh):

time: 121 us -> 113 us (0.934)
  Pallas kernels: 33.9 us -> 30.1 us
  waiting for transfers between devices: 14.7 us -> 12.7 us
  starting transfers between devices: 28 us -> 26.7 us
    all_to_all x4, waiting for transfers between devices: 12.9 us -> 9.08 us  [exchange(): return lax.all_to_all(block, axes, 0, 0, tiled=True)]
    pallas_call x1, Pallas kernels: 12.4 us -> 9.66 us  [scaled_inverse(): pl.pallas_call(functools.partial(scaled_inverse_kernel, float(total)), ou...]
    pallas_call x3 -> x5, Pallas kernels: 14.2 us -> 12 us  [the longest x1 9.12 us: gram_inverse(): pl.pallas_call(gram_inverse_kernel, out_shape=(square, square), in_specs=...]
    ppermute x7, waiting for transfers between devices: 1.76 us -> 3.64 us  [swap(): return lax.ppermute(block, 'op', [(0, 1), (1, 0)])]
  transfers between devices with their start and end apart: 11 -> 11, of which waited for: 4 -> 7; matrix products, arithmetic and copies ran while one was open for 2% -> 1% of each run, Pallas kernels for 26% -> 25%
where the time goes in v3:
time: 113 us; the launch traced here: 112 us
  blocking collectives  38.5 us (34%)
  Pallas kernels  30.1 us (27%)
  starting transfers between devices  26.7 us (24%)
  waiting for transfers between devices  12.7 us (11%)
  local copies, waits for them, and re-layouts  2.46 us (2%)
    all_to_all x3, blocking collectives, exchange(): return lax.all_to_all(block, axes, 0, 0, tiled=True)  38.5 us
    all_to_all x4, starting transfers between devices, exchange(): return lax.all_to_all(block, axes, 0, 0, tiled=True)  15.4 us
    ppermute x7, starting transfers between devices, swap(): return lax.ppermute(block, 'op', [(0, 1), (1, 0)])  11.3 us
    pallas_call x1, Pallas kernels, scaled_inverse(): pl.pallas_call(functools.partial(scaled_inverse_kernel, float(total)), ou...  9.66 us
    pallas_call x1, Pallas kernels, gram_inverse(): pl.pallas_call(gram_inverse_kernel, out_shape=(square, square), in_specs=...  9.12 us
    all_to_all x4, waiting for transfers between devices, exchange(): return lax.all_to_all(block, axes, 0, 0, tiled=True)  9.08 us
    pallas_call x1, Pallas kernels, second_product(): pl.pallas_call(second_product_kernel, out_shape=(part, part), in_specs=[S...  3.88 us
    ppermute x7, waiting for transfers between devices, swap(): return lax.ppermute(block, 'op', [(0, 1), (1, 0)])  3.64 us
  transfers between devices with their start and end apart: 11, of which 7 were waited for; matrix products, arithmetic and copies ran while one was open for 1% of the time, Pallas kernels for 25%

profile of v3, /device:TPU:1, one launch (start us, length us, event | category | flops | bytes accessed | tf_op | source)
XLA Modules:
  0.0 112.1 jit_solution(17022599812566136370)
XLA Ops:
  1.3 20.5 %all_to_all.35.mine_ref = bf16[16,16,256]{2,1,0:T(8,128)(2,1)S(1)} all-to-all(bf16[16,16,256]{2,1,0:T(8,128)(2,1)S(1)} %broadcast_in_dim.6), channel_id=1, replica_groups=mesh['freq'=16,'sens'=8,'op'=2] {'freq'}, dimensions={0} | all-to-all | bytes 262144 | tf_op jit(solution)/shard_map/all_to_all | solution.py:439
  21.8 1.1 broadcast_in_dim.15
  22.9 4.1 %all-to-all-start.2 = ((bf16[8,256,256]{2,1,0:T(8,128)(2,1)}), bf16[8,256,256]{2,1,0:T(8,128)(2,1)S(1)}, u32[]{:S(2)}, u32[]{:S(2)}) async-start(bf16[8,256,256]{2,1,0:T(8,128)(2,1)} %broadcast_in_dim.15), calls=%async_computation.2 | async-start | bytes 2097152 | tf_op jit(solution)/shard_map/all_to_all | solution.py:439
  27.0 2.4 %collective-permute-start = (bf16[16,16,256]{2,1,0:T(8,128)(2,1)S(1)}, bf16[16,16,256]{2,1,0:T(8,128)(2,1)S(1)}, u32[]{:S(2)}, u32[]{:S(2)}) collective-permute-start(bf16[16,16,256]{2,1,0:T(8,128)(2,1)S(1)} %all_to_all.35.mine_ref), channel_id=1, source_target_pairs={{0,1},{1,0},{2,3},{3,2},{4,5},{5,4},{6,7},{7,6},{8,9},{9,8},{10,11... | collective-permute-start | bytes 393224 | tf_op jit(solution)/shard_map/ppermute | solution.py:447
  29.5 0.9 collective-permute-done.other_ref
  31.1 3.6 %first_product.1 = (f32[8,64,256]{2,1,0:T(8,128)S(1)}, f32[8,64,256]{2,1,0:T(8,128)S(1)}) custom-call(s32[3]{0:T(128)S(1)} %pad_add_fusion.core_ref.place_ref, bf16[4,1024,512]{2,1,0:T(8,128)(2,1)} %tensor_ref.3, bf16[16,16,256]{2,1,0:T(8,128)(2,1)S(1)} %all_to_all.35.mine_ref, bf16[16,16,256]{2,1,0:T(8,128)(2,1)S(1)} %collective-permute-done.other_ref, ...), custom_call_target="tpu_custom_call" | custom-call | flops 2000000000 | bytes 6000000 | tf_op jit(solution)/shard_map/first_product/pallas_call | solution.py:248
  35.1 1.5 %collective-permute-done.1 = f32[8,64,256]{2,1,0:T(8,128)S(1)} collective-permute-done((f32[8,64,256]{2,1,0:T(8,128)S(1)}, f32[8,64,256]{2,1,0:T(8,128)S(1)}, u32[]{:S(2)}, u32[]{:S(2)}) %collective-permute-start.1) | collective-permute-done | bytes 524320 | tf_op jit(solution)/shard_map/ppermute | solution.py:447
  36.7 0.9 add.11.gate_ref
  37.5 3.2 %all-to-all-done.2.rows_ref = bf16[8,256,256]{2,1,0:T(8,128)(2,1)S(1)} async-done(((bf16[8,256,256]{2,1,0:T(8,128)(2,1)}), bf16[8,256,256]{2,1,0:T(8,128)(2,1)S(1)}, u32[]{:S(2)}, u32[]{:S(2)}) %all-to-all-start.2) | async-done | bytes 1048608 | tf_op jit(solution)/shard_map/all_to_all | solution.py:439
  41.3 2.9 %collective-permute-start.2 = (f32[2,256,256]{2,1,0:T(8,128)S(1)}, f32[2,256,256]{2,1,0:T(8,128)S(1)}, u32[]{:S(2)}, u32[]{:S(2)}) collective-permute-start(f32[2,256,256]{2,1,0:T(8,128)S(1)} %rows_grams.1.mine_ref), channel_id=1, source_target_pairs={{0,1},{1,0},{2,3},{3,2},{4,5},{5,4},{6,7},{7,6},{8,9},{9,8},{10,11... | collective-permute-start | bytes 1572872 | tf_op jit(solution)/shard_map/ppermute | solution.py:447
  44.2 3.5 %all-to-all-start.1 = ((f32[8,64,256]{2,1,0:T(8,128)}), f32[8,64,256]{2,1,0:T(8,128)S(1)}, u32[]{:S(2)}, u32[]{:S(2)}) async-start(f32[8,64,256]{2,1,0:T(8,128)} %add.11.gate_ref), calls=%async_computation.1 | async-start | bytes 1048576 | tf_op jit(solution)/shard_map/all_to_all | solution.py:439
  47.7 9.1 %gram_inverse.1 = (f32[256,256]{1,0:T(8,128)S(1)}, f32[256,256]{1,0:T(8,128)S(1)}) custom-call(f32[2,256,256]{2,1,0:T(8,128)S(1)} %rows_grams.1.mine_ref, f32[2,256,256]{2,1,0:T(8,128)S(1)} %collective-permute-done.2.other_ref), custom_call_target="tpu_custom_call" | custom-call | flops 20000000000 | bytes 1000000 | tf_op jit(solution)/shard_map/gram_inverse/pallas_call | solution.py:169
  57.6 10.3 %all_to_all.36.mine_ref.rows_ref = bf16[8,64,256]{2,1,0:T(8,128)(2,1)S(1)} all-to-all(bf16[8,64,256]{2,1,0:T(8,128)(2,1)S(1)} %get-tuple-element.17), channel_id=1, replica_groups=mesh['freq'=16,'sens'=8,'op'=2] {'sens'}, dimensions={0} | all-to-all | bytes 524288 | tf_op jit(solution)/shard_map/all_to_all | solution.py:439
  67.9 1.9 %collective-permute-start.3 = (bf16[8,64,256]{2,1,0:T(8,128)(2,1)S(1)}, bf16[8,64,256]{2,1,0:T(8,128)(2,1)S(1)}, u32[]{:S(2)}, u32[]{:S(2)}) collective-permute-start(bf16[8,64,256]{2,1,0:T(8,128)(2,1)S(1)} %all_to_all.36.mine_ref.rows_ref), channel_id=1, source_target_pairs={{0,1},{1,0},{2,3},{3,2},{4,5},{5,4},{6,7},{7,6},{8,9},{9,8},{10,11... | collective-permute-start | bytes 786440 | tf_op jit(solution)/shard_map/ppermute | solution.py:447
  70.7 1.2 %collective-permute-done.5.other_ref = f32[16,256]{1,0:T(8,128)S(1)} collective-permute-done((f32[16,256]{1,0:T(8,128)S(1)}, f32[16,256]{1,0:T(8,128)S(1)}, u32[]{:S(2)}, u32[]{:S(2)}) %collective-permute-start.5) | collective-permute-done | bytes 16416 | tf_op jit(solution)/shard_map/ppermute | solution.py:447
  72.6 3.9 %all-to-all-start.4 = ((bf16[16,16,256]{2,1,0:T(8,128)(2,1)}), bf16[16,16,256]{2,1,0:T(8,128)(2,1)S(1)}, u32[]{:S(2)}, u32[]{:S(2)}) async-start(bf16[16,16,256]{2,1,0:T(8,128)(2,1)} %pair_spread.1), calls=%async_computation.4 | async-start | bytes 262144 | tf_op jit(solution)/shard_map/all_to_all | solution.py:439
  76.5 3.9 %second_product.1 = (f32[16,16,256]{2,1,0:T(8,128)S(1)}, f32[16,16,256]{2,1,0:T(8,128)S(1)}) custom-call(s32[3]{0:T(128)S(1)} %pad_add_fusion.core_ref.place_ref, bf16[4,1024,512]{2,1,0:T(8,128)(2,1)} %tensor_ref.3, bf16[8,64,256]{2,1,0:T(8,128)(2,1)S(1)} %all_to_all.36.mine_ref.rows_ref, bf16[8,64,256]{2,1,0:T(8,128)(2,1)S(1)} %collective-permute-done.3.other_ref, ...), custom_call_target="tpu_custom_call" | custom-call | flops 2000000000 | bytes 6000000 | tf_op jit(solution)/shard_map/second_product/pallas_call | solution.py:297
  81.0 4.5 %all-to-all-done.4.parts_ref = bf16[16,16,256]{2,1,0:T(8,128)(2,1)S(1)} async-done(((bf16[16,16,256]{2,1,0:T(8,128)(2,1)}), bf16[16,16,256]{2,1,0:T(8,128)(2,1)S(1)}, u32[]{:S(2)}, u32[]{:S(2)}) %all-to-all-start.4) | async-done | bytes 131104 | tf_op jit(solution)/shard_map/all_to_all | solution.py:439
  85.5 7.7 %all_to_all.37.gate_ref.mine_ref = f32[8,16,256]{2,1,0:T(8,128)S(1)} all-to-all(f32[8,16,256]{2,1,0:T(8,128)S(1)} %sum_spread.1), channel_id=1, replica_groups=mesh['freq'=16,'sens'=8,'op'=2] {'sens'}, dimensions={0} | all-to-all | bytes 262144 | tf_op jit(solution)/shard_map/all_to_all | solution.py:439
  93.2 3.0 %collective-permute-start.6 = (f32[8,16,256]{2,1,0:T(8,128)S(1)}, f32[8,16,256]{2,1,0:T(8,128)S(1)}, u32[]{:S(2)}, u32[]{:S(2)}) collective-permute-start(f32[8,16,256]{2,1,0:T(8,128)S(1)} %all_to_all.37.gate_ref.mine_ref), channel_id=1, source_target_pairs={{0,1},{1,0},{2,3},{3,2},{4,5},{5,4},{6,7},{7,6},{8,9},{9,8},{10,11... | collective-permute-start | bytes 393224 | tf_op jit(solution)/shard_map/ppermute | solution.py:447
  96.9 3.8 %all-to-all-start.6 = ((f32[16,16,256]{2,1,0:T(8,128)}), f32[16,16,256]{2,1,0:T(8,128)S(1)}, u32[]{:S(2)}, u32[]{:S(2)}) async-start(f32[16,16,256]{2,1,0:T(8,128)} %add_after.1), calls=%async_computation.6 | async-start | bytes 524288 | tf_op jit(solution)/shard_map/all_to_all | solution.py:439
  100.7 9.7 %scaled_inverse.1 = (f32[256,256]{1,0:T(8,128)S(1)}, f32[8,256]{1,0:T(8,128)S(1)}) custom-call(s32[3]{0:T(128)S(1)} %pad_add_fusion.core_ref.place_ref, f32[8,16,256]{2,1,0:T(8,128)S(1)} %all_to_all.37.gate_ref.mine_ref, f32[8,16,256]{2,1,0:T(8,128)S(1)} %collective-permute-done.6.other_ref, f32[256,256]{1,0:T(8,128)S(1)} %get-tuple-element.23.c_ref), custom_call_target="tpu_custom_call" | custom-call | flops 20000000000 | bytes 1000000 | tf_op jit(solution)/shard_map/scaled_inverse/pallas_call | solution.py:201
  110.4 0.9 all-to-all-done.6.parts_ref
  111.2 0.8 last_rows.1
  (20 shorter events, 6.0 us)
Async XLA Ops:
  22.9 17.9 %all-to-all-start.2 = ((bf16[8,256,256]{2,1,0:T(8,128)(2,1)}), bf16[8,256,256]{2,1,0:T(8,128)(2,1)S(1)}, u32[]{:S(2)}, u32[]{:S(2)}) async-start(bf16[8,256,256]{2,1,0:T(8,128)(2,1)} %broadcast_in_dim.15), calls=%async_computation.2 | async-start | bytes 2097152 | tf_op jit(solution)/shard_map/all_to_all | solution.py:439
  27.0 3.4 %collective-permute-start = (bf16[16,16,256]{2,1,0:T(8,128)(2,1)S(1)}, bf16[16,16,256]{2,1,0:T(8,128)(2,1)S(1)}, u32[]{:S(2)}, u32[]{:S(2)}) collective-permute-start(bf16[16,16,256]{2,1,0:T(8,128)(2,1)S(1)} %all_to_all.35.mine_ref), channel_id=1, source_target_pairs={{0,1},{1,0},{2,3},{3,2},{4,5},{5,4},{6,7},{7,6},{8,9},{9,8},{10,11... | collective-permute-start | bytes 393224 | tf_op jit(solution)/shard_map/ppermute | solution.py:447
  30.4 0.7 copy-start
  31.1 9.7 %copy-start.1 = (bf16[4,256]{1,0:T(4,128)(2,1)S(1)}, bf16[4,256]{1,0:T(4,128)(2,1)}, u32[]{:S(2)}) copy-start(bf16[4,256]{1,0:T(4,128)(2,1)} %c_ref.5) | copy-start | bytes 6148
  34.7 2.0 %collective-permute-start.1 = (f32[8,64,256]{2,1,0:T(8,128)S(1)}, f32[8,64,256]{2,1,0:T(8,128)S(1)}, u32[]{:S(2)}, u32[]{:S(2)}) collective-permute-start(f32[8,64,256]{2,1,0:T(8,128)S(1)} %get-tuple-element.15), channel_id=1, source_target_pairs={{0,1},{1,0},{2,3},{3,2},{4,5},{5,4},{6,7},{7,6},{8,9},{9,8},{10,11... | collective-permute-start | bytes 1572872 | tf_op jit(solution)/shard_map/ppermute | solution.py:447
  41.3 6.4 %collective-permute-start.2 = (f32[2,256,256]{2,1,0:T(8,128)S(1)}, f32[2,256,256]{2,1,0:T(8,128)S(1)}, u32[]{:S(2)}, u32[]{:S(2)}) collective-permute-start(f32[2,256,256]{2,1,0:T(8,128)S(1)} %rows_grams.1.mine_ref), channel_id=1, source_target_pairs={{0,1},{1,0},{2,3},{3,2},{4,5},{5,4},{6,7},{7,6},{8,9},{9,8},{10,11... | collective-permute-start | bytes 1572872 | tf_op jit(solution)/shard_map/ppermute | solution.py:447
  44.2 13.1 %all-to-all-start.1 = ((f32[8,64,256]{2,1,0:T(8,128)}), f32[8,64,256]{2,1,0:T(8,128)S(1)}, u32[]{:S(2)}, u32[]{:S(2)}) async-start(f32[8,64,256]{2,1,0:T(8,128)} %add.11.gate_ref), calls=%async_computation.1 | async-start | bytes 1048576 | tf_op jit(solution)/shard_map/all_to_all | solution.py:439
  67.9 8.6 %collective-permute-start.3 = (bf16[8,64,256]{2,1,0:T(8,128)(2,1)S(1)}, bf16[8,64,256]{2,1,0:T(8,128)(2,1)S(1)}, u32[]{:S(2)}, u32[]{:S(2)}) collective-permute-start(bf16[8,64,256]{2,1,0:T(8,128)(2,1)S(1)} %all_to_all.36.mine_ref.rows_ref), channel_id=1, source_target_pairs={{0,1},{1,0},{2,3},{3,2},{4,5},{5,4},{6,7},{7,6},{8,9},{9,8},{10,11... | collective-permute-start | bytes 786440 | tf_op jit(solution)/shard_map/ppermute | solution.py:447
  70.6 1.3 %collective-permute-start.5 = (f32[16,256]{1,0:T(8,128)S(1)}, f32[16,256]{1,0:T(8,128)S(1)}, u32[]{:S(2)}, u32[]{:S(2)}) collective-permute-start(f32[16,256]{1,0:T(8,128)S(1)} %get-tuple-element.21), channel_id=1, source_target_pairs={{0,1},{1,0},{2,3},{3,2},{4,5},{5,4},{6,7},{7,6},{8,9},{9,8},{10,11... | collective-permute-start | bytes 49160 | tf_op jit(solution)/shard_map/ppermute | solution.py:447
  72.6 12.9 %all-to-all-start.4 = ((bf16[16,16,256]{2,1,0:T(8,128)(2,1)}), bf16[16,16,256]{2,1,0:T(8,128)(2,1)S(1)}, u32[]{:S(2)}, u32[]{:S(2)}) async-start(bf16[16,16,256]{2,1,0:T(8,128)(2,1)} %pair_spread.1), calls=%async_computation.4 | async-start | bytes 262144 | tf_op jit(solution)/shard_map/all_to_all | solution.py:439
  80.4 15.8 %collective-permute-start.4 = (f32[16,16,256]{2,1,0:T(8,128)S(1)}, f32[16,16,256]{2,1,0:T(8,128)S(1)}, u32[]{:S(2)}, u32[]{:S(2)}) collective-permute-start(f32[16,16,256]{2,1,0:T(8,128)S(1)} %get-tuple-element.19), channel_id=1, source_target_pairs={{0,1},{1,0},{2,3},{3,2},{4,5},{5,4},{6,7},{7,6},{8,9},{9,8},{10,11... | collective-permute-start | bytes 786440 | tf_op jit(solution)/shard_map/ppermute | solution.py:447
  93.2 7.5 %collective-permute-start.6 = (f32[8,16,256]{2,1,0:T(8,128)S(1)}, f32[8,16,256]{2,1,0:T(8,128)S(1)}, u32[]{:S(2)}, u32[]{:S(2)}) collective-permute-start(f32[8,16,256]{2,1,0:T(8,128)S(1)} %all_to_all.37.gate_ref.mine_ref), channel_id=1, source_target_pairs={{0,1},{1,0},{2,3},{3,2},{4,5},{5,4},{6,7},{7,6},{8,9},{9,8},{10,11... | collective-permute-start | bytes 393224 | tf_op jit(solution)/shard_map/ppermute | solution.py:447
  96.9 14.3 %all-to-all-start.6 = ((f32[16,16,256]{2,1,0:T(8,128)}), f32[16,16,256]{2,1,0:T(8,128)S(1)}, u32[]{:S(2)}, u32[]{:S(2)}) async-start(f32[16,16,256]{2,1,0:T(8,128)} %add_after.1), calls=%async_computation.6 | async-start | bytes 524288 | tf_op jit(solution)/shard_map/all_to_all | solution.py:439

commit v4 on v3

--- a/solution.py
+++ b/solution.py
@@ -41,20 +41,19 @@
         determinant = first * second - cross * cross
         guess = pl.reciprocal(determinant, approx=True)
         guess = guess * (2.0 - determinant * guess)
-        pp, qp, qq = second * guess, -(cross * guess), first * guess
         rest = [i for i in range(8) if i not in (p, q)]
         left = {i: entry(i, p) for i in rest}
         right = {i: entry(i, q) for i in rest}
-        left_new = {i: left[i] * pp + right[i] * qp for i in rest}
-        right_new = {i: left[i] * qp + right[i] * qq for i in rest}
+        left_new = {i: left[i] * second - right[i] * cross for i in rest}
+        right_new = {i: right[i] * first - left[i] * cross for i in rest}
         for i in rest:
             for j in rest:
                 if j <= i:
-                    d[i, j] = d[i, j] - (left_new[i] * left[j] + right_new[i] * right[j])
+                    d[i, j] = d[i, j] - (left_new[i] * left[j] + right_new[i] * right[j]) * guess
         for i in rest:
-            d[max(i, p), min(i, p)] = left_new[i]
-            d[max(i, q), min(i, q)] = right_new[i]
-        d[p, p], d[q, p], d[q, q] = -pp, -qp, -qq
+            d[max(i, p), min(i, p)] = left_new[i] * guess
+            d[max(i, q), min(i, q)] = right_new[i] * guess
+        d[p, p], d[q, p], d[q, q] = -(second * guess), cross * guess, -(first * guess)
     return entry
 
 
@@ -347,7 +346,7 @@
 
 def last_rows_kernel(parts_ref, raw_ref, inverse_ref, rows_ref, a_ref, b_ref):
     a_ref[...] = raw_ref[...] * (1.0 / rows_ref[2:3, :])
-    rows = jnp.sum(parts_ref[...], axis=0) * rows_ref[0:1, :]
+    rows = jnp.sum(parts_ref[...].astype(F32), axis=0) * rows_ref[0:1, :]
     b_ref[...] = dot(rows, inverse_ref[...]) * rows_ref[1:2, :]
 
 
@@ -421,13 +420,13 @@
 
 
 def add_after_kernel(keep_ref, received_ref, gate_ref, out_ref):
-    out_ref[...] = keep_ref[...] + received_ref[...]
+    out_ref[...] = (keep_ref[...] + received_ref[...]).astype(BF16)
 
 
 def add_after(keep, received, gate):
     return pl.pallas_call(
         add_after_kernel,
-        out_shape=jax.ShapeDtypeStruct(keep.shape, F32),
+        out_shape=jax.ShapeDtypeStruct(keep.shape, BF16),
         in_specs=[WHOLE, WHOLE, pl.BlockSpec(memory_space=pl.ANY)],
         out_specs=WHOLE,
         compiler_params=PARAMS,

time: 113 us -> 111 us (0.982)
  transfers between devices with their start and end apart: 11 -> 11, of which waited for: 7 -> 6; matrix products, arithmetic and copies ran while one was open for 1% -> 1% of each run, Pallas kernels for 25% -> 25%
where the time goes in v4:
time: 111 us
  blocking collectives  38.3 us (35%)
  Pallas kernels  29.7 us (27%)
  starting transfers between devices  26.7 us (24%)
  waiting for transfers between devices  12 us (11%)
  local copies, waits for them, and re-layouts  2.46 us (2%)
    all_to_all x3, blocking collectives, exchange(): return lax.all_to_all(block, axes, 0, 0, tiled=True)  38.3 us
    all_to_all x4, starting transfers between devices, exchange(): return lax.all_to_all(block, axes, 0, 0, tiled=True)  15.4 us
    ppermute x7, starting transfers between devices, swap(): return lax.ppermute(block, 'op', [(0, 1), (1, 0)])  11.3 us
    pallas_call x1, Pallas kernels, scaled_inverse(): pl.pallas_call(functools.partial(scaled_inverse_kernel, float(total)), ou...  9.5 us
    pallas_call x1, Pallas kernels, gram_inverse(): pl.pallas_call(gram_inverse_kernel, out_shape=(square, square), in_specs=...  8.96 us
    all_to_all x4, waiting for transfers between devices, exchange(): return lax.all_to_all(block, axes, 0, 0, tiled=True)  8.38 us
    pallas_call x1, Pallas kernels, second_product(): pl.pallas_call(second_product_kernel, out_shape=(part, part), in_specs=[S...  3.88 us
    ppermute x7, waiting for transfers between devices, swap(): return lax.ppermute(block, 'op', [(0, 1), (1, 0)])  3.64 us
  transfers between devices with their start and end apart: 11, of which 6 were waited for; matrix products, arithmetic and copies ran while one was open for 1% of the time, Pallas kernels for 25%

profile of v4, /device:TPU:1, one launch (start us, length us, event | category | flops | bytes accessed | tf_op | source)
XLA Modules:
  0.0 110.9 jit_solution(5757567756092714730)
XLA Ops:
  1.3 20.5 %all_to_all.35.mine_ref = bf16[16,16,256]{2,1,0:T(8,128)(2,1)S(1)} all-to-all(bf16[16,16,256]{2,1,0:T(8,128)(2,1)S(1)} %broadcast_in_dim.6), channel_id=1, replica_groups=mesh['freq'=16,'sens'=8,'op'=2] {'freq'}, dimensions={0} | all-to-all | bytes 262144 | tf_op jit(solution)/shard_map/all_to_all | solution.py:438
  21.8 1.1 broadcast_in_dim.15
  22.9 4.1 %all-to-all-start.2 = ((bf16[8,256,256]{2,1,0:T(8,128)(2,1)}), bf16[8,256,256]{2,1,0:T(8,128)(2,1)S(1)}, u32[]{:S(2)}, u32[]{:S(2)}) async-start(bf16[8,256,256]{2,1,0:T(8,128)(2,1)} %broadcast_in_dim.15), calls=%async_computation.2 | async-start | bytes 2097152 | tf_op jit(solution)/shard_map/all_to_all | solution.py:438
  27.0 2.4 %collective-permute-start = (bf16[16,16,256]{2,1,0:T(8,128)(2,1)S(1)}, bf16[16,16,256]{2,1,0:T(8,128)(2,1)S(1)}, u32[]{:S(2)}, u32[]{:S(2)}) collective-permute-start(bf16[16,16,256]{2,1,0:T(8,128)(2,1)S(1)} %all_to_all.35.mine_ref), channel_id=1, source_target_pairs={{0,1},{1,0},{2,3},{3,2},{4,5},{5,4},{6,7},{7,6},{8,9},{9,8},{10,11... | collective-permute-start | bytes 393224 | tf_op jit(solution)/shard_map/ppermute | solution.py:446
  29.5 0.9 collective-permute-done.other_ref
  31.1 3.6 %first_product.1 = (f32[8,64,256]{2,1,0:T(8,128)S(1)}, f32[8,64,256]{2,1,0:T(8,128)S(1)}) custom-call(s32[3]{0:T(128)S(1)} %pad_add_fusion.core_ref.place_ref, bf16[4,1024,512]{2,1,0:T(8,128)(2,1)} %tensor_ref.3, bf16[16,16,256]{2,1,0:T(8,128)(2,1)S(1)} %all_to_all.35.mine_ref, bf16[16,16,256]{2,1,0:T(8,128)(2,1)S(1)} %collective-permute-done.other_ref, ...), custom_call_target="tpu_custom_call" | custom-call | flops 2000000000 | bytes 6000000 | tf_op jit(solution)/shard_map/first_product/pallas_call | solution.py:247
  35.1 1.5 %collective-permute-done.1 = f32[8,64,256]{2,1,0:T(8,128)S(1)} collective-permute-done((f32[8,64,256]{2,1,0:T(8,128)S(1)}, f32[8,64,256]{2,1,0:T(8,128)S(1)}, u32[]{:S(2)}, u32[]{:S(2)}) %collective-permute-start.1) | collective-permute-done | bytes 524320 | tf_op jit(solution)/shard_map/ppermute | solution.py:446
  36.7 0.9 add.11.gate_ref
  37.5 3.2 %all-to-all-done.2.rows_ref = bf16[8,256,256]{2,1,0:T(8,128)(2,1)S(1)} async-done(((bf16[8,256,256]{2,1,0:T(8,128)(2,1)}), bf16[8,256,256]{2,1,0:T(8,128)(2,1)S(1)}, u32[]{:S(2)}, u32[]{:S(2)}) %all-to-all-start.2) | async-done | bytes 1048608 | tf_op jit(solution)/shard_map/all_to_all | solution.py:438
  41.3 2.9 %collective-permute-start.2 = (f32[2,256,256]{2,1,0:T(8,128)S(1)}, f32[2,256,256]{2,1,0:T(8,128)S(1)}, u32[]{:S(2)}, u32[]{:S(2)}) collective-permute-start(f32[2,256,256]{2,1,0:T(8,128)S(1)} %rows_grams.1.mine_ref), channel_id=1, source_target_pairs={{0,1},{1,0},{2,3},{3,2},{4,5},{5,4},{6,7},{7,6},{8,9},{9,8},{10,11... | collective-permute-start | bytes 1572872 | tf_op jit(solution)/shard_map/ppermute | solution.py:446
  44.2 3.5 %all-to-all-start.1 = ((f32[8,64,256]{2,1,0:T(8,128)}), f32[8,64,256]{2,1,0:T(8,128)S(1)}, u32[]{:S(2)}, u32[]{:S(2)}) async-start(f32[8,64,256]{2,1,0:T(8,128)} %add.11.gate_ref), calls=%async_computation.1 | async-start | bytes 1048576 | tf_op jit(solution)/shard_map/all_to_all | solution.py:438
  47.7 9.0 %gram_inverse.1 = (f32[256,256]{1,0:T(8,128)S(1)}, f32[256,256]{1,0:T(8,128)S(1)}) custom-call(f32[2,256,256]{2,1,0:T(8,128)S(1)} %rows_grams.1.mine_ref, f32[2,256,256]{2,1,0:T(8,128)S(1)} %collective-permute-done.2.other_ref), custom_call_target="tpu_custom_call" | custom-call | flops 20000000000 | bytes 1000000 | tf_op jit(solution)/shard_map/gram_inverse/pallas_call | solution.py:168
  57.6 10.2 %all_to_all.36.mine_ref.rows_ref = bf16[8,64,256]{2,1,0:T(8,128)(2,1)S(1)} all-to-all(bf16[8,64,256]{2,1,0:T(8,128)(2,1)S(1)} %get-tuple-element.17), channel_id=1, replica_groups=mesh['freq'=16,'sens'=8,'op'=2] {'sens'}, dimensions={0} | all-to-all | bytes 524288 | tf_op jit(solution)/shard_map/all_to_all | solution.py:438
  67.7 1.9 %collective-permute-start.3 = (bf16[8,64,256]{2,1,0:T(8,128)(2,1)S(1)}, bf16[8,64,256]{2,1,0:T(8,128)(2,1)S(1)}, u32[]{:S(2)}, u32[]{:S(2)}) collective-permute-start(bf16[8,64,256]{2,1,0:T(8,128)(2,1)S(1)} %all_to_all.36.mine_ref.rows_ref), channel_id=1, source_target_pairs={{0,1},{1,0},{2,3},{3,2},{4,5},{5,4},{6,7},{7,6},{8,9},{9,8},{10,11... | collective-permute-start | bytes 786440 | tf_op jit(solution)/shard_map/ppermute | solution.py:446
  69.7 0.8 gram_strips.1
  70.6 1.2 %collective-permute-done.5.other_ref = f32[16,256]{1,0:T(8,128)S(1)} collective-permute-done((f32[16,256]{1,0:T(8,128)S(1)}, f32[16,256]{1,0:T(8,128)S(1)}, u32[]{:S(2)}, u32[]{:S(2)}) %collective-permute-start.5) | collective-permute-done | bytes 16416 | tf_op jit(solution)/shard_map/ppermute | solution.py:446
  72.4 4.0 %all-to-all-start.4 = ((bf16[16,16,256]{2,1,0:T(8,128)(2,1)}), bf16[16,16,256]{2,1,0:T(8,128)(2,1)S(1)}, u32[]{:S(2)}, u32[]{:S(2)}) async-start(bf16[16,16,256]{2,1,0:T(8,128)(2,1)} %pair_spread.1), calls=%async_computation.4 | async-start | bytes 262144 | tf_op jit(solution)/shard_map/all_to_all | solution.py:438
  76.4 3.9 %second_product.1 = (f32[16,16,256]{2,1,0:T(8,128)S(1)}, f32[16,16,256]{2,1,0:T(8,128)S(1)}) custom-call(s32[3]{0:T(128)S(1)} %pad_add_fusion.core_ref.place_ref, bf16[4,1024,512]{2,1,0:T(8,128)(2,1)} %tensor_ref.3, bf16[8,64,256]{2,1,0:T(8,128)(2,1)S(1)} %all_to_all.36.mine_ref.rows_ref, bf16[8,64,256]{2,1,0:T(8,128)(2,1)S(1)} %collective-permute-done.3.other_ref, ...), custom_call_target="tpu_custom_call" | custom-call | flops 2000000000 | bytes 6000000 | tf_op jit(solution)/shard_map/second_product/pallas_call | solution.py:296
  80.8 4.5 %all-to-all-done.4.parts_ref = bf16[16,16,256]{2,1,0:T(8,128)(2,1)S(1)} async-done(((bf16[16,16,256]{2,1,0:T(8,128)(2,1)}), bf16[16,16,256]{2,1,0:T(8,128)(2,1)S(1)}, u32[]{:S(2)}, u32[]{:S(2)}) %all-to-all-start.4) | async-done | bytes 131104 | tf_op jit(solution)/shard_map/all_to_all | solution.py:438
  85.3 7.7 %all_to_all.37.gate_ref.mine_ref = f32[8,16,256]{2,1,0:T(8,128)S(1)} all-to-all(f32[8,16,256]{2,1,0:T(8,128)S(1)} %sum_spread.1), channel_id=1, replica_groups=mesh['freq'=16,'sens'=8,'op'=2] {'sens'}, dimensions={0} | all-to-all | bytes 262144 | tf_op jit(solution)/shard_map/all_to_all | solution.py:438
  93.0 3.0 %collective-permute-start.6 = (f32[8,16,256]{2,1,0:T(8,128)S(1)}, f32[8,16,256]{2,1,0:T(8,128)S(1)}, u32[]{:S(2)}, u32[]{:S(2)}) collective-permute-start(f32[8,16,256]{2,1,0:T(8,128)S(1)} %all_to_all.37.gate_ref.mine_ref), channel_id=1, source_target_pairs={{0,1},{1,0},{2,3},{3,2},{4,5},{5,4},{6,7},{7,6},{8,9},{9,8},{10,11... | collective-permute-start | bytes 393224 | tf_op jit(solution)/shard_map/ppermute | solution.py:446
  96.7 3.8 %all-to-all-start.6 = ((bf16[16,16,256]{2,1,0:T(8,128)(2,1)}), bf16[16,16,256]{2,1,0:T(8,128)(2,1)S(1)}, u32[]{:S(2)}, u32[]{:S(2)}) async-start(bf16[16,16,256]{2,1,0:T(8,128)(2,1)} %add_after.1), calls=%async_computation.6 | async-start | bytes 262144 | tf_op jit(solution)/shard_map/all_to_all | solution.py:438
  100.5 9.5 %scaled_inverse.1 = (f32[256,256]{1,0:T(8,128)S(1)}, f32[8,256]{1,0:T(8,128)S(1)}) custom-call(s32[3]{0:T(128)S(1)} %pad_add_fusion.core_ref.place_ref, f32[8,16,256]{2,1,0:T(8,128)S(1)} %all_to_all.37.gate_ref.mine_ref, f32[8,16,256]{2,1,0:T(8,128)S(1)} %collective-permute-done.6.other_ref, f32[256,256]{1,0:T(8,128)S(1)} %get-tuple-element.23.c_ref), custom_call_target="tpu_custom_call" | custom-call | flops 20000000000 | bytes 1000000 | tf_op jit(solution)/shard_map/scaled_inverse/pallas_call | solution.py:200
  110.0 0.9 last_rows.1
  (20 shorter events, 5.3 us)
Async XLA Ops:
  22.9 17.9 %all-to-all-start.2 = ((bf16[8,256,256]{2,1,0:T(8,128)(2,1)}), bf16[8,256,256]{2,1,0:T(8,128)(2,1)S(1)}, u32[]{:S(2)}, u32[]{:S(2)}) async-start(bf16[8,256,256]{2,1,0:T(8,128)(2,1)} %broadcast_in_dim.15), calls=%async_computation.2 | async-start | bytes 2097152 | tf_op jit(solution)/shard_map/all_to_all | solution.py:438
  27.0 3.4 %collective-permute-start = (bf16[16,16,256]{2,1,0:T(8,128)(2,1)S(1)}, bf16[16,16,256]{2,1,0:T(8,128)(2,1)S(1)}, u32[]{:S(2)}, u32[]{:S(2)}) collective-permute-start(bf16[16,16,256]{2,1,0:T(8,128)(2,1)S(1)} %all_to_all.35.mine_ref), channel_id=1, source_target_pairs={{0,1},{1,0},{2,3},{3,2},{4,5},{5,4},{6,7},{7,6},{8,9},{9,8},{10,11... | collective-permute-start | bytes 393224 | tf_op jit(solution)/shard_map/ppermute | solution.py:446
  30.4 0.7 copy-start
  31.1 9.7 %copy-start.1 = (bf16[4,256]{1,0:T(4,128)(2,1)S(1)}, bf16[4,256]{1,0:T(4,128)(2,1)}, u32[]{:S(2)}) copy-start(bf16[4,256]{1,0:T(4,128)(2,1)} %c_ref.5) | copy-start | bytes 6148
  34.7 2.0 %collective-permute-start.1 = (f32[8,64,256]{2,1,0:T(8,128)S(1)}, f32[8,64,256]{2,1,0:T(8,128)S(1)}, u32[]{:S(2)}, u32[]{:S(2)}) collective-permute-start(f32[8,64,256]{2,1,0:T(8,128)S(1)} %get-tuple-element.15), channel_id=1, source_target_pairs={{0,1},{1,0},{2,3},{3,2},{4,5},{5,4},{6,7},{7,6},{8,9},{9,8},{10,11... | collective-permute-start | bytes 1572872 | tf_op jit(solution)/shard_map/ppermute | solution.py:446
  41.3 6.4 %collective-permute-start.2 = (f32[2,256,256]{2,1,0:T(8,128)S(1)}, f32[2,256,256]{2,1,0:T(8,128)S(1)}, u32[]{:S(2)}, u32[]{:S(2)}) collective-permute-start(f32[2,256,256]{2,1,0:T(8,128)S(1)} %rows_grams.1.mine_ref), channel_id=1, source_target_pairs={{0,1},{1,0},{2,3},{3,2},{4,5},{5,4},{6,7},{7,6},{8,9},{9,8},{10,11... | collective-permute-start | bytes 1572872 | tf_op jit(solution)/shard_map/ppermute | solution.py:446
  44.2 13.1 %all-to-all-start.1 = ((f32[8,64,256]{2,1,0:T(8,128)}), f32[8,64,256]{2,1,0:T(8,128)S(1)}, u32[]{:S(2)}, u32[]{:S(2)}) async-start(f32[8,64,256]{2,1,0:T(8,128)} %add.11.gate_ref), calls=%async_computation.1 | async-start | bytes 1048576 | tf_op jit(solution)/shard_map/all_to_all | solution.py:438
  67.7 8.6 %collective-permute-start.3 = (bf16[8,64,256]{2,1,0:T(8,128)(2,1)S(1)}, bf16[8,64,256]{2,1,0:T(8,128)(2,1)S(1)}, u32[]{:S(2)}, u32[]{:S(2)}) collective-permute-start(bf16[8,64,256]{2,1,0:T(8,128)(2,1)S(1)} %all_to_all.36.mine_ref.rows_ref), channel_id=1, source_target_pairs={{0,1},{1,0},{2,3},{3,2},{4,5},{5,4},{6,7},{7,6},{8,9},{9,8},{10,11... | collective-permute-start | bytes 786440 | tf_op jit(solution)/shard_map/ppermute | solution.py:446
  70.5 1.3 %collective-permute-start.5 = (f32[16,256]{1,0:T(8,128)S(1)}, f32[16,256]{1,0:T(8,128)S(1)}, u32[]{:S(2)}, u32[]{:S(2)}) collective-permute-start(f32[16,256]{1,0:T(8,128)S(1)} %get-tuple-element.21), channel_id=1, source_target_pairs={{0,1},{1,0},{2,3},{3,2},{4,5},{5,4},{6,7},{7,6},{8,9},{9,8},{10,11... | collective-permute-start | bytes 49160 | tf_op jit(solution)/shard_map/ppermute | solution.py:446
  72.4 12.9 %all-to-all-start.4 = ((bf16[16,16,256]{2,1,0:T(8,128)(2,1)}), bf16[16,16,256]{2,1,0:T(8,128)(2,1)S(1)}, u32[]{:S(2)}, u32[]{:S(2)}) async-start(bf16[16,16,256]{2,1,0:T(8,128)(2,1)} %pair_spread.1), calls=%async_computation.4 | async-start | bytes 262144 | tf_op jit(solution)/shard_map/all_to_all | solution.py:438
  80.3 15.7 %collective-permute-start.4 = (f32[16,16,256]{2,1,0:T(8,128)S(1)}, f32[16,16,256]{2,1,0:T(8,128)S(1)}, u32[]{:S(2)}, u32[]{:S(2)}) collective-permute-start(f32[16,16,256]{2,1,0:T(8,128)S(1)} %get-tuple-element.19), channel_id=1, source_target_pairs={{0,1},{1,0},{2,3},{3,2},{4,5},{5,4},{6,7},{7,6},{8,9},{9,8},{10,11... | collective-permute-start | bytes 786440 | tf_op jit(solution)/shard_map/ppermute | solution.py:446
  93.0 7.5 %collective-permute-start.6 = (f32[8,16,256]{2,1,0:T(8,128)S(1)}, f32[8,16,256]{2,1,0:T(8,128)S(1)}, u32[]{:S(2)}, u32[]{:S(2)}) collective-permute-start(f32[8,16,256]{2,1,0:T(8,128)S(1)} %all_to_all.37.gate_ref.mine_ref), channel_id=1, source_target_pairs={{0,1},{1,0},{2,3},{3,2},{4,5},{5,4},{6,7},{7,6},{8,9},{9,8},{10,11... | collective-permute-start | bytes 393224 | tf_op jit(solution)/shard_map/ppermute | solution.py:446
  96.7 13.3 %all-to-all-start.6 = ((bf16[16,16,256]{2,1,0:T(8,128)(2,1)}), bf16[16,16,256]{2,1,0:T(8,128)(2,1)S(1)}, u32[]{:S(2)}, u32[]{:S(2)}) async-start(bf16[16,16,256]{2,1,0:T(8,128)(2,1)} %add_after.1), calls=%async_computation.6 | async-start | bytes 262144 | tf_op jit(solution)/shard_map/all_to_all | solution.py:438
